TPU v7x, 128 devices: a whole 4x4x4 slice. The times are simulated.
128 devices in a mesh: dev: 128 (over x, z, y, core).
Axes of the slice: x: 4, y: 4, z: 4, core: 2. Of those that a mesh axis runs over, the one named last changes fastest.
Arguments:
- gauss_params: float32 [59, 1048576], P(None, 'dev'), may hold values from -8 to 8, as said below
- adam_first: float32 [59, 1048576], P(None, 'dev'), may hold values from -6 to 6
- adam_second: float32 [59, 1048576], P(None, 'dev'), may hold values from 0.0001 to 100
- camera: float32 [2, 6], replicated, may hold values from -0.004 to 0.004
- send_first: int32 [128, 4096], P('dev'), may hold values from -1 to 8191, as said below
- send_second: int32 [128, 4096], P('dev'), may hold values from -1 to 8191, as said below
- lists_first: int32 [4096, 128], P('dev'), may hold values from -1 to 4095, as said below
- lists_second: int32 [4096, 128], P('dev'), may hold values from -1 to 4095, as said below
- tiles_first: int32 [4096], P('dev'), may hold values from 0 to 4095, as said below
- tiles_second: int32 [4096], P('dev'), may hold values from 0 to 4095, as said below
- targets: float32 [4096, 3, 256], P('dev'), may hold values from 0 to 1
Outputs:
- new_params: float32 [59, 1048576], P(None, 'dev')
- new_first: float32 [59, 1048576], P(None, 'dev')
- new_second: float32 [59, 1048576], P(None, 'dev')
- rendered_next: float32 [4096, 3, 256], P('dev')
Inputs may be any that keep to these rules, and one draw needn't show every extreme that they name: `gauss_params`: rows 0 to 2 hold a position, 3 to 5 log scales, 6 to 9 a quaternion (w, x, y, z) with w at least 1, 10 an opacity logit, 11 + 16 c + k the spherical-harmonic coefficient k of colour c. Every Gaussian lies at depth 1.4 or more in front of both cameras. `send_first`: row s holds, for each destination d in turn, 32 slots: local column indices of Gaussians of device s, the used ones first, then -1. Entries other than -1 in a row are distinct. Some destination gets 32 used slots from every device. `send_second`: same form as send_first, but unused slots (-1) may stand anywhere in a destination's run. Some destination gets 32 used slots from every device. `lists_first`: row r, rendered by device r // 32, lists in compositing order (front first) received slots s * 32 + k of that device (slot k from device s), only used slots, then -1 to the end. Every used slot of a device appears exactly once among its rows. Some rows have no -1. `lists_second`: same form as lists_first, for the next view and its send array. `tiles_first`: A permutation of the image's tiles. `tiles_second`: A permutation of the image's tiles.
All inputs are finite; a program needn't handle non-finite values.
Results may differ from a plain program's by a relative error of at most 0.0003.
Values sent between devices are 32-bit elements; how exact they have to be, the bound alone decides.
A program may use at most 128 MiB of HBM per device.

v0:
```python
import functools

import jax
import jax.numpy as jnp
import numpy as np
from jax import lax
from jax.experimental import pallas as pl
from jax.experimental.pallas import tpu as pltpu
from jax.sharding import PartitionSpec as P

LANES = 128
TILES_X = 128
TILE_DEV = 32
LIST_LEN = 128
CHUNK = 1024
LOG2E = 1.4426950408889634

focal_length = 1000.0
blur_floor = 0.3
adam_epsilon = 1e-08
bias_first = 1.0 - 0.9**20
bias_second = 1.0 - 0.999**20
sh_first = 0.28209479177387814
sh_second = 0.4886025119029199
sh_third = (
    1.0925484305920792,
    -1.0925484305920792,
    0.31539156525252005,
    -1.0925484305920792,
    0.5462742152960396,
)
sh_fourth = (
    -0.5900435899266435,
    2.890611442640554,
    -0.4570457994644658,
    0.3731763325901154,
    -0.4570457994644658,
    1.445305721320277,
    -0.5900435899266435,
)


def rate_values():
    values = np.full((64,), 0.000125)
    values[0:3] = 0.00016
    values[3:6] = 0.005
    values[6:10] = 0.001
    values[10] = 0.05
    values[11] = 0.0025
    values[27] = 0.0025
    values[43] = 0.0025
    return np.broadcast_to(values[:, None], (64, LANES)).astype(np.float32)


def camera_frame(camera_ref, view):
    def full(k):
        return jnp.full((8, LANES), camera_ref[view, k], jnp.float32)

    ca, sa = jnp.cos(full(0)), jnp.sin(full(0))
    cb, sb = jnp.cos(full(1)), jnp.sin(full(1))
    cc, sc = jnp.cos(full(2)), jnp.sin(full(2))
    rot = [
        [cc * cb, cc * (sb * sa) - sc * ca, cc * (sb * ca) + sc * sa],
        [sc * cb, sc * (sb * sa) + cc * ca, sc * (sb * ca) - cc * sa],
        [-sb, cb * sa, cb * ca],
    ]
    shift = [full(3), full(4), full(5)]
    back = [rot[0][k] * shift[0] + rot[1][k] * shift[1] + rot[2][k] * shift[2] for k in range(3)]
    return [rot[0][0], rot[0][1], rot[0][2], rot[1][0], rot[1][1], rot[1][2],
            rot[2][0], rot[2][1], rot[2][2]] + shift + back


def sh_terms(along_x, along_y, along_z):
    square_x, square_y, square_z = (along_x * along_x, along_y * along_y, along_z * along_z)
    return [
        -sh_second * along_y,
        sh_second * along_z,
        -sh_second * along_x,
        sh_third[0] * along_x * along_y,
        sh_third[1] * along_y * along_z,
        sh_third[2] * (2.0 * square_z - square_x - square_y),
        sh_third[3] * along_x * along_z,
        sh_third[4] * (square_x - square_y),
        sh_fourth[0] * along_y * (3.0 * square_x - square_y),
        sh_fourth[1] * along_x * along_y * along_z,
        sh_fourth[2] * along_y * (4.0 * square_z - square_x - square_y),
        sh_fourth[3] * along_z * (2.0 * square_z - 3.0 * square_x - 3.0 * square_y),
        sh_fourth[4] * along_x * (4.0 * square_z - square_x - square_y),
        sh_fourth[5] * along_z * (square_x - square_y),
        sh_fourth[6] * along_x * (square_x - 3.0 * square_y),
    ]


def footprint(params, frame, half_width, half_height):
    rot = [frame[0:3], frame[3:6], frame[6:9]]
    shift, back = frame[9:12], frame[12:15]
    x, y, z = params[0], params[1], params[2]
    viewed = [rot[k][0] * x + rot[k][1] * y + rot[k][2] * z + shift[k] for k in range(3)]
    inverse_depth = 1.0 / viewed[2]
    screen_u = focal_length * viewed[0] * inverse_depth + half_width
    screen_v = focal_length * viewed[1] * inverse_depth + half_height
    scales = [jnp.exp(params[3 + k]) for k in range(3)]
    size = params[6] * params[6] + params[7] * params[7] + params[8] * params[8] + params[9] * params[9]
    unit = 1.0 / jnp.sqrt(size)
    w, i, j, k = [params[6 + n] * unit for n in range(4)]
    turn = [
        [1.0 - 2.0 * (j * j + k * k), 2.0 * (i * j - w * k), 2.0 * (i * k + w * j)],
        [2.0 * (i * j + w * k), 1.0 - 2.0 * (i * i + k * k), 2.0 * (j * k - w * i)],
        [2.0 * (i * k - w * j), 2.0 * (j * k + w * i), 1.0 - 2.0 * (i * i + j * j)],
    ]
    near = focal_length * inverse_depth
    slant_x = -near * viewed[0] * inverse_depth
    slant_y = -near * viewed[1] * inverse_depth
    mapping = [
        [near * rot[0][n] + slant_x * rot[2][n] for n in range(3)],
        [near * rot[1][n] + slant_y * rot[2][n] for n in range(3)],
    ]
    half = [
        [
            (mapping[m][0] * turn[0][n] + mapping[m][1] * turn[1][n] + mapping[m][2] * turn[2][n])
            * scales[n]
            for n in range(3)
        ]
        for m in range(2)
    ]

    def inner(p, q):
        return p[0] * q[0] + p[1] * q[1] + p[2] * q[2]

    cover_a = inner(half[0], half[0]) + blur_floor
    cover_b = inner(half[0], half[1])
    cover_c = inner(half[1], half[1]) + blur_floor
    towards = [x + back[0], y + back[1], z + back[2]]
    inverse_length = 1.0 / jnp.sqrt(inner(towards, towards))
    harmonics = sh_terms(*[t * inverse_length for t in towards])
    colours = []
    for channel in range(3):
        running = 0.5 + sh_first * params[11 + 16 * channel]
        for term in range(1, 16):
            running = running + harmonics[term - 1] * params[11 + 16 * channel + term]
        colours.append(jnp.maximum(running, 0.0))
    return (screen_u, screen_v, cover_a, cover_b, cover_c, *colours)


def conic_of(cover_a, cover_b, cover_c):
    inverse = 1.0 / (cover_a * cover_c - cover_b * cover_b)
    return cover_c * inverse, -cover_b * inverse, cover_a * inverse


def project(params, frame, half_width, half_height):
    u, w, cover_a, cover_b, cover_c, *colours = footprint(params, frame, half_width, half_height)
    return [u, w, *conic_of(cover_a, cover_b, cover_c), jax.nn.sigmoid(params[10]), *colours]


def turned(tiles):
    swapped = jnp.swapaxes(jnp.stack(tiles, axis=0), 0, 1)
    return [swapped[n] for n in range(8)]


def lane_pick(values, lanes):
    numbers = lax.GatherDimensionNumbers(
        offset_dims=(),
        collapsed_slice_dims=(1,),
        start_index_map=(1,),
        operand_batching_dims=(0,),
        start_indices_batching_dims=(0,),
    )
    return lax.gather(
        values, lanes[:, :, None], numbers, (1, 1), mode=lax.GatherScatterMode.PROMISE_IN_BOUNDS
    )


def pick(source_ref, blocks, wanted, unroll):
    count = source_ref.shape[0]
    high = [w >> 7 for w in wanted]
    low = [w & 127 for w in wanted]

    def body(block, held):
        hit = [h == block for h in high]
        out = []
        for row in range(count):
            source = jnp.broadcast_to(source_ref[row, pl.ds(block, 1), :], (8, LANES))
            for n in range(len(wanted)):
                out.append(
                    jnp.where(hit[n], lane_pick(source, low[n]), held[row * len(wanted) + n])
                )
        return tuple(out)

    start = tuple(jnp.zeros((8, LANES), jnp.float32) for _ in range(count * len(wanted)))
    flat = lax.fori_loop(0, blocks, body, start, unroll=unroll)
    return [list(flat[r * len(wanted) : (r + 1) * len(wanted)]) for r in range(count)]


def lane_block():
    return lax.broadcasted_iota(jnp.int32, (8, LANES), 1) >> 5


def block_turn(vectors):
    block = lane_block()
    out = []
    for j in range(4):
        made = None
        for i in range(4):
            shift = ((i - j) * 32) % LANES
            moved = pltpu.roll(vectors[i], shift, 1) if shift else vectors[i]
            made = moved if made is None else jnp.where(block == i, moved, made)
        out.append(made)
    return out


def pack(values, message_ref):
    nothing = jnp.zeros((8, LANES), jnp.float32)
    for g in range(4):
        for a in range(3):
            rows = [values[4 * a + b][g] if 4 * a + b < 9 else nothing for b in range(4)]
            for d, made in enumerate(block_turn(rows)):
                message_ref[8 * g : 8 * g + 8, d, a, :] = made
        for d in range(4):
            message_ref[8 * g : 8 * g + 8, d, 3, :] = nothing


def unpack(message_ref, buffer_ref):
    for g in range(4):
        for a in range(3):
            rows = [message_ref[8 * g : 8 * g + 8, d, a, :] for d in range(4)]
            for b, made in enumerate(block_turn(rows)):
                if 4 * a + b < 9:
                    buffer_ref[4 * a + b, 8 * g : 8 * g + 8, :] = made


def eight(ref, g):
    return ref[8 * g : 8 * g + 8, :]


def send_splats(splats_ref, send_ref, message_ref):
    picked = pick(splats_ref, splats_ref.shape[1], [eight(send_ref, g) for g in range(4)], 2)
    pack(picked, message_ref)


def first_kernel(camera_ref, params_ref, send_ref, message_ref, splats_ref, frame_ref, *, half):
    step = pl.program_id(0)

    @pl.when(step == 0)
    def _():
        for n, entry in enumerate(camera_frame(camera_ref, 0)):
            frame_ref[n] = entry

    rows = []
    for g in range(8):
        rows += turned([params_ref[8 * g : 8 * g + 8, LANES * c : LANES * (c + 1)] for c in range(8)])
    splats = project(rows, [frame_ref[n] for n in range(15)], *half)
    at = pl.ds(pl.multiple_of(step * 8, 8), 8)
    for n in range(9):
        splats_ref[n, at, :] = splats[n]

    @pl.when(step == pl.num_programs(0) - 1)
    def _():
        send_splats(splats_ref, send_ref, message_ref)


def inverse_of(ids_ref, blocks):
    lane = lax.broadcasted_iota(jnp.int32, (blocks, LANES), 1)
    row_id = lax.broadcasted_iota(jnp.int32, (blocks, LANES), 0)
    low_id = lax.broadcasted_iota(jnp.int32, (LANES, LANES), 0)
    lane_digit = (lane + 1).astype(jnp.float32)

    def body(j, total):
        ids = ids_ref[pl.ds(j, 1), :]
        hit = row_id == (ids >> 7)
        digit = jnp.full((blocks, LANES), j, jnp.int32).astype(jnp.float32)
        left = jnp.concatenate(
            [jnp.where(hit, lane_digit, 0.0), jnp.where(hit, digit, 0.0)], axis=0
        ).astype(jnp.bfloat16)
        right = jnp.where(low_id == (ids & 127), 1.0, 0.0).astype(jnp.bfloat16)
        return total + lax.dot_general(
            left, right, (((1,), (1,)), ((), ())), preferred_element_type=jnp.float32
        )

    total = lax.fori_loop(0, ids_ref.shape[0], body, jnp.zeros((2 * blocks, LANES), jnp.float32), unroll=4)
    return (total[blocks:] * 128.0 + total[:blocks]).astype(jnp.int32) - 1


def inverse_kernel(lists_ref, send_ref, from_list_ref, from_send_ref):
    from_list_ref[...] = inverse_of(lists_ref, from_list_ref.shape[0])
    from_send_ref[...] = inverse_of(send_ref, from_send_ref.shape[0])


def entry_rows(picked, rows_ref):
    block = lane_block()
    scale = {2: -0.5 * LOG2E, 3: -LOG2E, 4: -0.5 * LOG2E}
    for row in range(9):
        for g in range(4):
            value = picked[row][g]
            if row in scale:
                value = value * scale[row]
            moved = [value] + [pltpu.roll(value, 32 * k, 1) for k in range(1, 4)]
            for part in range(4):
                made = moved[(0 - part) % 4]
                for b in range(1, 4):
                    made = jnp.where(block == b, moved[(b - part) % 4], made)
                rows_ref[4 * row + part, 8 * g : 8 * g + 8, :] = made


def pixel_places(tiles_ref):
    lane = lax.broadcasted_iota(jnp.int32, (8, LANES), 1)
    sub = lax.broadcasted_iota(jnp.int32, (8, LANES), 0)
    tiles = jnp.broadcast_to(tiles_ref[0:1, :], (8, LANES))
    column = (tiles & (TILES_X - 1)) * 16 + sub
    row = (tiles >> 7) * 16 + (lane >> 5) * 4
    across = [column.astype(jnp.float32) + (0.5 + 8 * p) for p in range(2)]
    down = [row.astype(jnp.float32) + (0.5 + q) for q in range(4)]
    return across, down


def splat_at(rows_ref, j, part):
    return [
        jnp.broadcast_to(rows_ref[4 * row + part, pl.ds(j, 1), :], (8, LANES)) for row in range(9)
    ]


def composite(rows_ref, across, down, keep):
    def body(j, carry):
        clear, light = list(carry[:8]), [list(carry[8 + 8 * c : 16 + 8 * c]) for c in range(3)]
        for part in range(4):
            u, w, a, b, c2, o, *colour = splat_at(rows_ref, j, part)
            dx = [u - x for x in across]
            dy = [w - y for y in down]
            ax = [a * d for d in dx]
            by = [b * d for d in dy]
            cy = [c2 * d * d for d in dy]
            for v in range(8):
                q, p = v // 2, v % 2
                alpha = o * jnp.exp2((ax[p] + by[q]) * dx[p] + cy[q])
                weight = clear[v] * alpha
                if keep is not None:
                    keep[0][j, part * 8 + v] = alpha
                    keep[1][j, part * 8 + v] = weight
                clear[v] = clear[v] - weight
                for c in range(3):
                    light[c][v] = light[c][v] + colour[c] * weight
        return (*clear, *light[0], *light[1], *light[2])

    start = tuple([jnp.ones((8, LANES), jnp.float32)] * 8 + [jnp.zeros((8, LANES), jnp.float32)] * 24)
    done = lax.fori_loop(0, LIST_LEN // 4, body, start)
    return [done[8 + 8 * c : 16 + 8 * c] for c in range(3)]


def train_kernel(
    message_ref, lists_ref, inverse_ref, tiles_ref, targets_ref, back_ref,
    buffer_ref, rows_ref, alpha_ref, weight_ref, sums_ref, miss_ref,
):
    unpack(message_ref, buffer_ref)
    picked = pick(buffer_ref, 32, [eight(lists_ref, g) for g in range(4)], 2)
    entry_rows(picked, rows_ref)
    across, down = pixel_places(tiles_ref)
    light = composite(rows_ref, across, down, (alpha_ref, weight_ref))
    for c in range(3):
        for v in range(8):
            miss_ref[8 * c + v] = light[c][v] - targets_ref[c, 8 * v : 8 * v + 8, :]

    def body(step, behind):
        j = LIST_LEN // 4 - 1 - step
        behind = list(behind)
        for part in (3, 2, 1, 0):
            u, w, _, _, _, _, *colour = splat_at(rows_ref, j, part)
            dx = [u - x for x in across]
            dy = [w - y for y in down]
            pull = []
            tint = [None] * 3
            for v in range(8):
                alpha = alpha_ref[j, part * 8 + v]
                weight = weight_ref[j, part * 8 + v]
                miss = [miss_ref[8 * c + v] for c in range(3)]
                ahead = colour[0] * miss[0] + colour[1] * miss[1] + colour[2] * miss[2] - behind[v]
                pull.append(weight * ahead)
                behind[v] = behind[v] + alpha * ahead
                for c in range(3):
                    term = weight * miss[c]
                    tint[c] = term if tint[c] is None else tint[c] + term
            row_pull = [pull[2 * q] + pull[2 * q + 1] for q in range(4)]
            row_down = [row_pull[q] * dy[q] for q in range(4)]
            col_pull = [pull[p] + pull[2 + p] + pull[4 + p] + pull[6 + p] for p in range(2)]
            col_down = [
                pull[p] * dy[0] + pull[2 + p] * dy[1] + pull[4 + p] * dy[2] + pull[6 + p] * dy[3]
                for p in range(2)
            ]
            col_across = [col_pull[p] * dx[p] for p in range(2)]
            sums = [
                col_across[0] + col_across[1],
                row_down[0] + row_down[1] + row_down[2] + row_down[3],
                col_across[0] * dx[0] + col_across[1] * dx[1],
                col_down[0] * dx[0] + col_down[1] * dx[1],
                row_down[0] * dy[0] + row_down[1] * dy[1] + row_down[2] * dy[2] + row_down[3] * dy[3],
                col_pull[0] + col_pull[1],
                *tint,
            ]
            for n in range(9):
                sums_ref[4 * n + part, pl.ds(j, 1), :] = jnp.sum(sums[n], axis=0, keepdims=True)
        return tuple(behind)

    lax.fori_loop(0, LIST_LEN // 4, body, tuple([jnp.zeros((8, LANES), jnp.float32)] * 8))

    block = lane_block()
    for g in range(4):
        moment = []
        for n in range(9):
            made = None
            for part in range(4):
                value = sums_ref[4 * n + part, 8 * g : 8 * g + 8, :]
                value = value + pltpu.roll(value, 64, 1)
                value = value + pltpu.roll(value, 32, 1)
                made = value if made is None else jnp.where(block == part, value, made)
            moment.append(made)
        a, b, c2 = picked[2][g], picked[3][g], picked[4][g]
        grads = [
            -(a * moment[0] + b * moment[1]),
            -(c2 * moment[1] + b * moment[0]),
            -0.5 * moment[2],
            -moment[3],
            -0.5 * moment[4],
            *moment[5:],
        ]
        for n in range(9):
            buffer_ref[n, 8 * g : 8 * g + 8, :] = grads[n]
    returned = pick(buffer_ref, 32, [eight(inverse_ref, g) for g in range(4)], 2)
    pack(returned, back_ref)


def update_kernel(
    camera_ref, rates_ref, back_ref, inverse_ref, send_ref, params_ref, first_ref, second_ref,
    new_params_ref, new_first_ref, new_second_ref, message_ref,
    buffer_ref, splats_ref, frame_ref, *, half,
):
    step = pl.program_id(0)

    @pl.when(step == 0)
    def _():
        unpack(back_ref, buffer_ref)
        for view in range(2):
            for n, entry in enumerate(camera_frame(camera_ref, view)):
                frame_ref[view, n] = entry

    slot_grads = [g[0] for g in pick(buffer_ref, 32, [inverse_ref[...]], 4)]
    rows = []
    for g in range(8):
        rows += turned([params_ref[8 * g : 8 * g + 8, LANES * c : LANES * (c + 1)] for c in range(8)])
    frame = [frame_ref[0, n] for n in range(15)]
    used = rows[:10] + [None] + rows[11:59]

    def view_first(*leaves):
        return footprint(list(leaves[:10]) + [None] + list(leaves[10:]), frame, *half)

    made, pullback = jax.vjp(view_first, *(used[:10] + used[11:]))
    ka, kb, kc = conic_of(*made[2:5])
    ga, gb, gc = slot_grads[2], 0.5 * slot_grads[3], slot_grads[4]
    left = [[ka * ga + kb * gb, ka * gb + kb * gc], [kb * ga + kc * gb, kb * gb + kc * gc]]
    cover_grads = (
        -(left[0][0] * ka + left[0][1] * kb),
        -2.0 * (left[0][0] * kb + left[0][1] * kc),
        -(left[1][0] * kb + left[1][1] * kc),
    )
    grads = list(pullback((slot_grads[0], slot_grads[1], *cover_grads, *slot_grads[6:])))
    opacity_grad = slot_grads[5] * (1.0 - jax.nn.sigmoid(rows[10]))
    grads = grads[:10] + [opacity_grad] + grads[10:] + [jnp.zeros((8, LANES), jnp.float32)] * 5
    new_rows = []
    for g in range(8):
        columns = turned(grads[8 * g : 8 * g + 8])
        rate = rates_ref[8 * g : 8 * g + 8, :]
        fresh = []
        for c in range(8):
            at = (slice(8 * g, 8 * g + 8), slice(LANES * c, LANES * (c + 1)))
            gradient = columns[c]
            first = 0.9 * first_ref[at] + 0.1 * gradient
            second = 0.999 * second_ref[at] + 0.001 * gradient * gradient
            value = params_ref[at] - rate * (first * (1.0 / bias_first)) / (
                jnp.sqrt(second * (1.0 / bias_second)) + adam_epsilon
            )
            new_first_ref[at] = first
            new_second_ref[at] = second
            new_params_ref[at] = value
            fresh.append(value)
        new_rows += turned(fresh)
    splats = project(new_rows, [frame_ref[1, n] for n in range(15)], *half)
    at = pl.ds(pl.multiple_of(step * 8, 8), 8)
    for n in range(9):
        splats_ref[n, at, :] = splats[n]

    @pl.when(step == pl.num_programs(0) - 1)
    def _():
        send_splats(splats_ref, send_ref, message_ref)


def render_kernel(message_ref, lists_ref, tiles_ref, image_ref, buffer_ref, rows_ref):
    unpack(message_ref, buffer_ref)
    picked = pick(buffer_ref, 32, [eight(lists_ref, g) for g in range(4)], 2)
    entry_rows(picked, rows_ref)
    across, down = pixel_places(tiles_ref)
    light = composite(rows_ref, across, down, None)
    for c in range(3):
        flat = jnp.concatenate(list(light[c]), axis=0)
        upright = jnp.transpose(jnp.concatenate([flat, flat], axis=0))
        pieces = [upright[32 * b : 32 * b + 32, :] for b in range(4)]
        low = lax.broadcasted_iota(jnp.int32, (32, LANES), 1) < 64
        image_ref[:, c, 0:128] = jnp.where(low, pieces[0], pieces[1])
        image_ref[:, c, 128:256] = jnp.where(low, pieces[2], pieces[3])


def vmem(shape):
    return pltpu.VMEM(shape, jnp.float32)


def whole():
    return pl.BlockSpec(memory_space=pltpu.VMEM)


def scalars():
    return pl.BlockSpec(memory_space=pltpu.SMEM)


def f32(*shape):
    return jax.ShapeDtypeStruct(shape, jnp.float32)


def exchange(message, axis):
    flat = message.reshape(-1, 4, LANES)
    return lax.all_to_all(flat, axis, 0, 0, tiled=True).reshape(message.shape)


def shards(
    gauss_params, adam_first, adam_second, camera, send_first, send_second,
    lists_first, lists_second, tiles_first, tiles_second, targets,
):
    local = gauss_params.shape[1]
    steps = local // CHUNK
    half = (TILES_X * 8.0, lists_first.shape[0] * lax.axis_size("dev") // TILES_X * 8.0)
    limit = pltpu.CompilerParams(vmem_limit_bytes=48 * 1024 * 1024)
    slots_first, slots_second = send_first.reshape(32, LANES), send_second.reshape(32, LANES)
    order_first = lists_first.T.reshape(32, LANES)
    order_second = lists_second.T.reshape(32, LANES)
    places_first = jnp.tile(tiles_first, 4)[None]
    places_second = jnp.tile(tiles_second, 4)[None]
    goals = jnp.transpose(targets.reshape(TILE_DEV, 3, 4, 64), (1, 3, 2, 0)).reshape(3, 64, LANES)
    block = pl.BlockSpec((64, CHUNK), lambda i: (0, i))
    fixed = pl.BlockSpec((32, LANES), lambda i: (0, 0))
    packet = pl.BlockSpec((32, 4, 4, LANES), lambda i: (0, 0, 0, 0))


    message = pl.pallas_call(
        functools.partial(first_kernel, half=half),
        grid=(steps,),
        out_shape=f32(32, 4, 4, LANES),
        in_specs=[scalars(), block, fixed],
        out_specs=packet,
        scratch_shapes=[vmem((9, local // LANES, LANES)), vmem((15, 8, LANES))],
        compiler_params=limit,
        name="project_first",
    )(camera, gauss_params, slots_first)
    received = exchange(message, "dev")
    from_list, from_send = pl.pallas_call(
        inverse_kernel,
        out_shape=(
            jax.ShapeDtypeStruct((32, LANES), jnp.int32),
            jax.ShapeDtypeStruct((local // LANES, LANES), jnp.int32),
        ),
        in_specs=[whole(), whole()],
        out_specs=(whole(), whole()),
        compiler_params=limit,
        name="inverses",
    )(order_first, slots_first)
    back = pl.pallas_call(
        train_kernel,
        out_shape=f32(32, 4, 4, LANES),
        in_specs=[whole()] * 5,
        out_specs=whole(),
        scratch_shapes=[
            vmem((9, 32, LANES)), vmem((36, 32, LANES)), vmem((32, 32, 8, LANES)),
            vmem((32, 32, 8, LANES)), vmem((36, 32, LANES)), vmem((24, 8, LANES)),
        ],
        compiler_params=limit,
        name="train",
    )(received, order_first, from_list, places_first, goals)
    returned = exchange(back, "dev")
    new_params, new_first, new_second, message_next = pl.pallas_call(
        functools.partial(update_kernel, half=half),
        grid=(steps,),
        out_shape=(f32(59, local), f32(59, local), f32(59, local), f32(32, 4, 4, LANES)),
        in_specs=[
            scalars(),
            pl.BlockSpec((64, LANES), lambda i: (0, 0)),
            packet,
            pl.BlockSpec((8, LANES), lambda i: (i, 0)),
            fixed,
            block, block, block,
        ],
        out_specs=(block, block, block, packet),
        scratch_shapes=[vmem((9, 32, LANES)), vmem((9, local // LANES, LANES)), vmem((2, 15, 8, LANES))],
        compiler_params=limit,
        name="update",
    )(camera, jnp.asarray(rate_values()), returned, from_send, slots_second, gauss_params, adam_first, adam_second)
    received_next = exchange(message_next, "dev")
    image = pl.pallas_call(
        render_kernel,
        out_shape=f32(TILE_DEV, 3, 256),
        in_specs=[whole()] * 3,
        out_specs=whole(),
        scratch_shapes=[vmem((9, 32, LANES)), vmem((36, 32, LANES))],
        compiler_params=limit,
        name="render",
    )(received_next, order_second, places_second)
    return (new_params, new_first, new_second, image)


def solution(mesh):
    split = P(None, "dev")
    rows = P("dev", None)
    return jax.shard_map(
        shards,
        mesh=mesh,
        in_specs=(split, split, split, P(), rows, rows, rows, rows, P("dev"), P("dev"), P("dev", None, None)),
        out_specs=(split, split, split, P("dev", None, None)),
        check_vma=False,
    )
```

profile of v0, /device:TPU:1, one launch (start us, length us, event | category | flops | bytes accessed | tf_op | source)
XLA Modules:
  0.0 116.9 jit_solution(10612297788670482771)
XLA Ops:
  0.6 0.0 copy-start.12
  0.6 0.0 copy-start
  0.7 1.6 %copy-done = f32[59,8192]{1,0:T(8,128)S(1)} copy-done((f32[59,8192]{1,0:T(8,128)S(1)}, f32[59,8192]{1,0:T(8,128)}, u32[]{:S(2)}) %copy-start) | copy-done | bytes 1933336
  2.2 0.0 copy-start.3
  2.2 0.7 copy-done.3
  3.0 0.0 copy-start.7
  3.0 0.7 copy-done.7
  3.6 0.0 copy-start.10
  3.6 0.0 copy-start.4
  3.6 0.0 copy-start.9
  3.6 0.0 copy-start.1
  3.6 0.0 copy-start.5
  3.7 0.0 copy-start.6
  3.7 0.0 copy-start.8
  3.7 11.2 %project_first.1 = f32[32,4,4,128]{3,2,1,0:T(4,128)} custom-call(f32[2,6]{1,0:T(2,128)S(1)} %copy-done.7, f32[59,8192]{1,0:T(8,128)S(1)} %copy-done, s32[32,128]{1,0:T(8,128)S(1)} %bitcast.19), custom_call_target="tpu_custom_call" | custom-call | tf_op jit(solution)/shard_map/project_first/pallas_call | solution.py:548
  14.8 11.5 %all-to-all-start = ((f32[128,4,128]{2,1,0:T(4,128)}), f32[128,4,128]{2,1,0:T(4,128)S(1)}, u32[]{:S(2)}, u32[]{:S(2)}) async-start(f32[128,4,128]{2,1,0:T(4,128)} %bitcast.1), calls=%async_computation | async-start | bytes 524288 | tf_op jit(solution)/shard_map/all_to_all | solution.py:526
  26.3 0.0 copy-done.10
  26.3 0.1 copy.20
  26.4 0.1 reshape.49.lists_ref
  26.5 0.0 copy-done.4
  26.5 3.3 %inverses.1 = (s32[32,128]{1,0:T(8,128)S(1)}, s32[64,128]{1,0:T(8,128)S(1)}) custom-call(s32[32,128]{1,0:T(8,128)S(1)} %reshape.49.lists_ref, s32[32,128]{1,0:T(8,128)S(1)} %bitcast.20), custom_call_target="tpu_custom_call" | custom-call | tf_op jit(solution)/shard_map/inverses/pallas_call | solution.py:559
  29.9 0.0 copy-done.9
  29.9 0.1 reshape.50
  30.1 0.1 copy.22.targets_ref
  30.2 0.0 copy-done.12
  30.2 0.1 broadcast_in_dim_tile.6.tiles_ref
  30.3 6.8 %all-to-all-done = f32[128,4,128]{2,1,0:T(4,128)S(1)} async-done(((f32[128,4,128]{2,1,0:T(4,128)}), f32[128,4,128]{2,1,0:T(4,128)S(1)}, u32[]{:S(2)}, u32[]{:S(2)}) %all-to-all-start) | async-done | bytes 262176 | tf_op jit(solution)/shard_map/all_to_all | solution.py:526
  37.1 16.8 %train.1 = f32[32,4,4,128]{3,2,1,0:T(4,128)S(1)} custom-call(f32[32,4,4,128]{3,2,1,0:T(4,128)S(1)} %bitcast.17, s32[32,128]{1,0:T(8,128)S(1)} %reshape.49.lists_ref, s32[32,128]{1,0:T(8,128)S(1)} %get-tuple-element.10.inverse_ref, s32[1,128]{1,0:T(1,128)S(1)} %broadcast_in_dim_tile.6.tiles_ref, f32[3,64,128]{2,1,0:T(8,128)S(1)} %copy.22.targets_ref), custom_call_target="tpu_custom_call" | custom-call | tf_op jit(solution)/shard_map/train/pallas_call | solution.py:570
  54.0 15.5 %all_to_all.15 = f32[128,4,128]{2,1,0:T(4,128)S(1)} all-to-all(f32[128,4,128]{2,1,0:T(4,128)S(1)} %bitcast.18), channel_id=1, replica_groups=mesh['dev'=128] {'dev'}, dimensions={0} | all-to-all | bytes 524288 | tf_op jit(solution)/shard_map/all_to_all | solution.py:526
  69.4 0.0 copy-done.1
  69.4 0.0 copy-done.5
  69.4 0.0 copy-done.6
  69.4 0.0 copy-done.8
  69.4 0.0 copy-start.2
  69.5 1.6 %copy-done.2 = f32[59,8192]{1,0:T(8,128)S(1)} copy-done((f32[59,8192]{1,0:T(8,128)S(1)}, f32[59,8192]{1,0:T(8,128)}, u32[]{:S(2)}) %copy-start.2) | copy-done | bytes 1933336
  71.0 0.0 copy-start.11
  71.0 0.0 copy-start.13
  71.0 22.3 %update.1 = (f32[59,8192]{1,0:T(8,128)}, f32[59,8192]{1,0:T(8,128)}, f32[59,8192]{1,0:T(8,128)}, f32[32,4,4,128]{3,2,1,0:T(4,128)}) custom-call(f32[2,6]{1,0:T(2,128)S(1)} %copy-done.8, f32[64,128]{1,0:T(8,128)S(1)} %copy-done.5, f32[32,4,4,128]{3,2,1,0:T(4,128)S(1)} %bitcast.15, s32[64,128]{1,0:T(8,128)S(1)} %get-tuple-element.11.inverse_ref, ...), custom_call_target="tpu_custom_call" | custom-call | tf_op jit(solution)/shard_map/update/pallas_call | solution.py:583
  93.3 4.7 %all-to-all-start.2 = ((f32[128,4,128]{2,1,0:T(4,128)}), f32[128,4,128]{2,1,0:T(4,128)S(1)}, u32[]{:S(2)}, u32[]{:S(2)}) async-start(f32[128,4,128]{2,1,0:T(4,128)} %bitcast.9), calls=%async_computation.2 | async-start | bytes 524288 | tf_op jit(solution)/shard_map/all_to_all | solution.py:526
  98.0 0.0 copy-done.11
  98.0 0.1 copy.23
  98.1 0.1 reshape.57.lists_ref
  98.2 0.0 copy-done.13
  98.2 0.1 broadcast_in_dim_tile.7.tiles_ref
  98.3 10.5 %all-to-all-done.2 = f32[128,4,128]{2,1,0:T(4,128)S(1)} async-done(((f32[128,4,128]{2,1,0:T(4,128)}), f32[128,4,128]{2,1,0:T(4,128)S(1)}, u32[]{:S(2)}, u32[]{:S(2)}) %all-to-all-start.2) | async-done | bytes 262176 | tf_op jit(solution)/shard_map/all_to_all | solution.py:526
  108.8 7.5 %render.1 = f32[32,3,256]{2,1,0:T(4,128)S(1)} custom-call(f32[32,4,4,128]{3,2,1,0:T(4,128)S(1)} %bitcast.16, s32[32,128]{1,0:T(8,128)S(1)} %reshape.57.lists_ref, s32[1,128]{1,0:T(1,128)S(1)} %broadcast_in_dim_tile.7.tiles_ref), custom_call_target="tpu_custom_call" | custom-call | tf_op jit(solution)/shard_map/render/pallas_call | solution.py:601
  116.3 0.7 copy.24
  (3 shorter events, 0.0 us)
Async XLA Ops:
  0.6 29.5 %copy-start.12 = (s32[32]{0:T(128)S(1)}, s32[32]{0:T(128)}, u32[]{:S(2)}) copy-start(s32[32]{0:T(128)} %param.20) | copy-start | bytes 388
  0.6 1.6 %copy-start = (f32[59,8192]{1,0:T(8,128)S(1)}, f32[59,8192]{1,0:T(8,128)}, u32[]{:S(2)}) copy-start(f32[59,8192]{1,0:T(8,128)} %params_ref.3) | copy-start | bytes 5799940
  2.2 0.7 copy-start.3
  3.0 0.7 copy-start.7
  3.6 22.7 %copy-start.10 = (s32[32,128]{1,0:T(8,128)S(1)}, s32[32,128]{1,0:T(8,128)}, u32[]{:S(2)}) copy-start(s32[32,128]{1,0:T(8,128)} %param.18) | copy-start | bytes 49156
  3.6 22.9 %copy-start.4 = (s32[1,4096]{1,0:T(1,128)S(1)}, s32[1,4096]{1,0:T(1,128)}, u32[]{:S(2)}) copy-start(s32[1,4096]{1,0:T(1,128)} %param.16) | copy-start | bytes 49156
  3.6 26.2 %copy-start.9 = (f32[32,3,256]{2,0,1:T(8,128)S(1)}, f32[32,3,256]{2,0,1:T(8,128)}, u32[]{:S(2)}) copy-start(f32[32,3,256]{2,0,1:T(8,128)} %param.22) | copy-start | bytes 294916
  3.6 65.8 %copy-start.1 = (f32[59,8192]{1,0:T(8,128)S(1)}, f32[59,8192]{1,0:T(8,128)}, u32[]{:S(2)}) copy-start(f32[59,8192]{1,0:T(8,128)} %params_ref.3) | copy-start | bytes 5799940
  3.6 65.8 %copy-start.5 = (f32[64,128]{1,0:T(8,128)S(1)}, f32[64,128]{1,0:T(8,128)}, u32[]{:S(2)}) copy-start(f32[64,128]{1,0:T(8,128)} %constant.2.clone.rates_ref) | copy-start | bytes 98308
  3.7 65.8 %copy-start.6 = (s32[1,4096]{1,0:T(1,128)S(1)}, s32[1,4096]{1,0:T(1,128)}, u32[]{:S(2)}) copy-start(s32[1,4096]{1,0:T(1,128)} %param.17) | copy-start | bytes 49156
  3.7 65.8 %copy-start.8 = (f32[2,6]{1,0:T(2,128)S(1)}, f32[2,6]{1,0:T(2,128)}, u32[]{:S(2)}) copy-start(f32[2,6]{1,0:T(2,128)} %camera_ref.3) | copy-start | bytes 148
  14.8 22.3 %all-to-all-start = ((f32[128,4,128]{2,1,0:T(4,128)}), f32[128,4,128]{2,1,0:T(4,128)S(1)}, u32[]{:S(2)}, u32[]{:S(2)}) async-start(f32[128,4,128]{2,1,0:T(4,128)} %bitcast.1), calls=%async_computation | async-start | bytes 524288 | tf_op jit(solution)/shard_map/all_to_all | solution.py:526
  69.4 1.6 %copy-start.2 = (f32[59,8192]{1,0:T(8,128)S(1)}, f32[59,8192]{1,0:T(8,128)}, u32[]{:S(2)}) copy-start(f32[59,8192]{1,0:T(8,128)} %first_ref.1) | copy-start | bytes 5799940
  71.0 26.9 %copy-start.11 = (s32[32,128]{1,0:T(8,128)S(1)}, s32[32,128]{1,0:T(8,128)}, u32[]{:S(2)}) copy-start(s32[32,128]{1,0:T(8,128)} %param.19) | copy-start | bytes 49156
  71.0 27.1 %copy-start.13 = (s32[32]{0:T(128)S(1)}, s32[32]{0:T(128)}, u32[]{:S(2)}) copy-start(s32[32]{0:T(128)} %param.21) | copy-start | bytes 388
  93.3 15.4 %all-to-all-start.2 = ((f32[128,4,128]{2,1,0:T(4,128)}), f32[128,4,128]{2,1,0:T(4,128)S(1)}, u32[]{:S(2)}, u32[]{:S(2)}) async-start(f32[128,4,128]{2,1,0:T(4,128)} %bitcast.9), calls=%async_computation.2 | async-start | bytes 524288 | tf_op jit(solution)/shard_map/all_to_all | solution.py:526
where the time goes:
time: 117 us
  Pallas kernels  61.1 us (52%)
  waiting for transfers between devices  17.3 us (15%)
  starting transfers between devices  16.1 us (14%)
  blocking collectives  15.5 us (13%)
  local copies, waits for them, and re-layouts  6.06 us (5%)
    pallas_call x1, Pallas kernels, shards(): pl.pallas_call(functools.partial(update_kernel, half=half), grid=(steps,)...  22.3 us
    all_to_all x2, waiting for transfers between devices, exchange(): return lax.all_to_all(flat, axis, 0, 0, tiled=True).reshape(message.shape)  17.3 us
    pallas_call x1, Pallas kernels, shards(): pl.pallas_call(train_kernel, out_shape=f32(32, 4, 4, LANES), in_specs=[wh...  16.8 us
    all_to_all x2, starting transfers between devices, exchange(): return lax.all_to_all(flat, axis, 0, 0, tiled=True).reshape(message.shape)  16.1 us
    all_to_all x1, blocking collectives, exchange(): return lax.all_to_all(flat, axis, 0, 0, tiled=True).reshape(message.shape)  15.5 us
    pallas_call x1, Pallas kernels, shards(): pl.pallas_call(functools.partial(first_kernel, half=half), grid=(steps,),...  11.2 us
    pallas_call x1, Pallas kernels, shards(): pl.pallas_call(render_kernel, out_shape=f32(TILE_DEV, 3, 256), in_specs=[...  7.49 us
    unnamed x29, local copies, waits for them, and re-layouts  5.28 us
  transfers between devices with their start and end apart: 2, of which 2 were waited for; matrix products, arithmetic and copies ran while one was open for 1% of the time, Pallas kernels for 3%

commit v1 on v0

--- a/solution.py
+++ b/solution.py
@@ -170,25 +170,26 @@
     )
 
 
-def pick(source_ref, blocks, wanted, unroll):
-    count = source_ref.shape[0]
-    high = [w >> 7 for w in wanted]
-    low = [w & 127 for w in wanted]
-
-    def body(block, held):
-        hit = [h == block for h in high]
-        out = []
+def pick_eight(source_ref, wanted):
+    count, blocks = source_ref.shape[:2]
+    high, low = wanted >> 7, wanted & 127
+    held = [jnp.zeros((8, LANES), jnp.float32)] * count
+    for block in range(blocks):
+        hit = high == block
         for row in range(count):
-            source = jnp.broadcast_to(source_ref[row, pl.ds(block, 1), :], (8, LANES))
-            for n in range(len(wanted)):
-                out.append(
-                    jnp.where(hit[n], lane_pick(source, low[n]), held[row * len(wanted) + n])
-                )
-        return tuple(out)
-
-    start = tuple(jnp.zeros((8, LANES), jnp.float32) for _ in range(count * len(wanted)))
-    flat = lax.fori_loop(0, blocks, body, start, unroll=unroll)
-    return [list(flat[r * len(wanted) : (r + 1) * len(wanted)]) for r in range(count)]
+            source = jnp.broadcast_to(source_ref[row, block : block + 1, :], (8, LANES))
+            held[row] = jnp.where(hit, lane_pick(source, low), held[row])
+    return held
+
+
+def pick(source_ref, wanted_ref, picked_ref):
+    def body(g, _):
+        at = pl.ds(pl.multiple_of(g * 8, 8), 8)
+        for row, value in enumerate(pick_eight(source_ref, wanted_ref[at, :])):
+            picked_ref[row, at, :] = value
+        return 0
+
+    lax.fori_loop(0, wanted_ref.shape[0] // 8, body, 0)
 
 
 def lane_block():
@@ -208,11 +209,14 @@
     return out
 
 
-def pack(values, message_ref):
+def pack(picked_ref, message_ref):
     nothing = jnp.zeros((8, LANES), jnp.float32)
     for g in range(4):
         for a in range(3):
-            rows = [values[4 * a + b][g] if 4 * a + b < 9 else nothing for b in range(4)]
+            rows = [
+                picked_ref[4 * a + b, 8 * g : 8 * g + 8, :] if 4 * a + b < 9 else nothing
+                for b in range(4)
+            ]
             for d, made in enumerate(block_turn(rows)):
                 message_ref[8 * g : 8 * g + 8, d, a, :] = made
         for d in range(4):
@@ -228,16 +232,14 @@
                     buffer_ref[4 * a + b, 8 * g : 8 * g + 8, :] = made
 
 
-def eight(ref, g):
-    return ref[8 * g : 8 * g + 8, :]
-
-
-def send_splats(splats_ref, send_ref, message_ref):
-    picked = pick(splats_ref, splats_ref.shape[1], [eight(send_ref, g) for g in range(4)], 2)
-    pack(picked, message_ref)
-
-
-def first_kernel(camera_ref, params_ref, send_ref, message_ref, splats_ref, frame_ref, *, half):
+def send_splats(splats_ref, send_ref, picked_ref, message_ref):
+    pick(splats_ref, send_ref, picked_ref)
+    pack(picked_ref, message_ref)
+
+
+def first_kernel(
+    camera_ref, params_ref, send_ref, message_ref, splats_ref, picked_ref, frame_ref, *, half
+):
     step = pl.program_id(0)
 
     @pl.when(step == 0)
@@ -255,7 +257,7 @@
 
     @pl.when(step == pl.num_programs(0) - 1)
     def _():
-        send_splats(splats_ref, send_ref, message_ref)
+        send_splats(splats_ref, send_ref, picked_ref, message_ref)
 
 
 def inverse_of(ids_ref, blocks):
@@ -285,12 +287,12 @@
     from_send_ref[...] = inverse_of(send_ref, from_send_ref.shape[0])
 
 
-def entry_rows(picked, rows_ref):
+def entry_rows(picked_ref, rows_ref):
     block = lane_block()
     scale = {2: -0.5 * LOG2E, 3: -LOG2E, 4: -0.5 * LOG2E}
     for row in range(9):
         for g in range(4):
-            value = picked[row][g]
+            value = picked_ref[row, 8 * g : 8 * g + 8, :]
             if row in scale:
                 value = value * scale[row]
             moved = [value] + [pltpu.roll(value, 32 * k, 1) for k in range(1, 4)]
@@ -347,11 +349,11 @@
 
 def train_kernel(
     message_ref, lists_ref, inverse_ref, tiles_ref, targets_ref, back_ref,
-    buffer_ref, rows_ref, alpha_ref, weight_ref, sums_ref, miss_ref,
+    buffer_ref, picked_ref, rows_ref, alpha_ref, weight_ref, sums_ref, miss_ref,
 ):
     unpack(message_ref, buffer_ref)
-    picked = pick(buffer_ref, 32, [eight(lists_ref, g) for g in range(4)], 2)
-    entry_rows(picked, rows_ref)
+    pick(buffer_ref, lists_ref, picked_ref)
+    entry_rows(picked_ref, rows_ref)
     across, down = pixel_places(tiles_ref)
     light = composite(rows_ref, across, down, (alpha_ref, weight_ref))
     for c in range(3):
@@ -411,7 +413,7 @@
                 value = value + pltpu.roll(value, 32, 1)
                 made = value if made is None else jnp.where(block == part, value, made)
             moment.append(made)
-        a, b, c2 = picked[2][g], picked[3][g], picked[4][g]
+        a, b, c2 = [picked_ref[n, 8 * g : 8 * g + 8, :] for n in (2, 3, 4)]
         grads = [
             -(a * moment[0] + b * moment[1]),
             -(c2 * moment[1] + b * moment[0]),
@@ -422,14 +424,14 @@
         ]
         for n in range(9):
             buffer_ref[n, 8 * g : 8 * g + 8, :] = grads[n]
-    returned = pick(buffer_ref, 32, [eight(inverse_ref, g) for g in range(4)], 2)
-    pack(returned, back_ref)
+    pick(buffer_ref, inverse_ref, picked_ref)
+    pack(picked_ref, back_ref)
 
 
 def update_kernel(
     camera_ref, rates_ref, back_ref, inverse_ref, send_ref, params_ref, first_ref, second_ref,
     new_params_ref, new_first_ref, new_second_ref, message_ref,
-    buffer_ref, splats_ref, frame_ref, *, half,
+    buffer_ref, splats_ref, picked_ref, frame_ref, *, half,
 ):
     step = pl.program_id(0)
 
@@ -440,7 +442,7 @@
             for n, entry in enumerate(camera_frame(camera_ref, view)):
                 frame_ref[view, n] = entry
 
-    slot_grads = [g[0] for g in pick(buffer_ref, 32, [inverse_ref[...]], 4)]
+    slot_grads = pick_eight(buffer_ref, inverse_ref[...])
     rows = []
     for g in range(8):
         rows += turned([params_ref[8 * g : 8 * g + 8, LANES * c : LANES * (c + 1)] for c in range(8)])
@@ -487,13 +489,13 @@
 
     @pl.when(step == pl.num_programs(0) - 1)
     def _():
-        send_splats(splats_ref, send_ref, message_ref)
-
-
-def render_kernel(message_ref, lists_ref, tiles_ref, image_ref, buffer_ref, rows_ref):
+        send_splats(splats_ref, send_ref, picked_ref, message_ref)
+
+
+def render_kernel(message_ref, lists_ref, tiles_ref, image_ref, buffer_ref, picked_ref, rows_ref):
     unpack(message_ref, buffer_ref)
-    picked = pick(buffer_ref, 32, [eight(lists_ref, g) for g in range(4)], 2)
-    entry_rows(picked, rows_ref)
+    pick(buffer_ref, lists_ref, picked_ref)
+    entry_rows(picked_ref, rows_ref)
     across, down = pixel_places(tiles_ref)
     light = composite(rows_ref, across, down, None)
     for c in range(3):
@@ -501,8 +503,8 @@
         upright = jnp.transpose(jnp.concatenate([flat, flat], axis=0))
         pieces = [upright[32 * b : 32 * b + 32, :] for b in range(4)]
         low = lax.broadcasted_iota(jnp.int32, (32, LANES), 1) < 64
-        image_ref[:, c, 0:128] = jnp.where(low, pieces[0], pieces[1])
-        image_ref[:, c, 128:256] = jnp.where(low, pieces[2], pieces[3])
+        image_ref[c, :, 0:128] = jnp.where(low, pieces[0], pieces[1])
+        image_ref[c, :, 128:256] = jnp.where(low, pieces[2], pieces[3])
 
 
 def vmem(shape):
@@ -534,6 +536,7 @@
     steps = local // CHUNK
     half = (TILES_X * 8.0, lists_first.shape[0] * lax.axis_size("dev") // TILES_X * 8.0)
     limit = pltpu.CompilerParams(vmem_limit_bytes=48 * 1024 * 1024)
+    streamed = pltpu.CompilerParams(vmem_limit_bytes=62 * 1024 * 1024)
     slots_first, slots_second = send_first.reshape(32, LANES), send_second.reshape(32, LANES)
     order_first = lists_first.T.reshape(32, LANES)
     order_second = lists_second.T.reshape(32, LANES)
@@ -551,8 +554,8 @@
         out_shape=f32(32, 4, 4, LANES),
         in_specs=[scalars(), block, fixed],
         out_specs=packet,
-        scratch_shapes=[vmem((9, local // LANES, LANES)), vmem((15, 8, LANES))],
-        compiler_params=limit,
+        scratch_shapes=[vmem((9, local // LANES, LANES)), vmem((9, 32, LANES)), vmem((15, 8, LANES))],
+        compiler_params=streamed,
         name="project_first",
     )(camera, gauss_params, slots_first)
     received = exchange(message, "dev")
@@ -573,7 +576,7 @@
         in_specs=[whole()] * 5,
         out_specs=whole(),
         scratch_shapes=[
-            vmem((9, 32, LANES)), vmem((36, 32, LANES)), vmem((32, 32, 8, LANES)),
+            vmem((9, 32, LANES)), vmem((9, 32, LANES)), vmem((36, 32, LANES)), vmem((32, 32, 8, LANES)),
             vmem((32, 32, 8, LANES)), vmem((36, 32, LANES)), vmem((24, 8, LANES)),
         ],
         compiler_params=limit,
@@ -593,21 +596,21 @@
             block, block, block,
         ],
         out_specs=(block, block, block, packet),
-        scratch_shapes=[vmem((9, 32, LANES)), vmem((9, local // LANES, LANES)), vmem((2, 15, 8, LANES))],
-        compiler_params=limit,
+        scratch_shapes=[vmem((9, 32, LANES)), vmem((9, local // LANES, LANES)), vmem((9, 32, LANES)), vmem((2, 15, 8, LANES))],
+        compiler_params=streamed,
         name="update",
     )(camera, jnp.asarray(rate_values()), returned, from_send, slots_second, gauss_params, adam_first, adam_second)
     received_next = exchange(message_next, "dev")
     image = pl.pallas_call(
         render_kernel,
-        out_shape=f32(TILE_DEV, 3, 256),
+        out_shape=f32(3, TILE_DEV, 256),
         in_specs=[whole()] * 3,
         out_specs=whole(),
-        scratch_shapes=[vmem((9, 32, LANES)), vmem((36, 32, LANES))],
+        scratch_shapes=[vmem((9, 32, LANES)), vmem((9, 32, LANES)), vmem((36, 32, LANES))],
         compiler_params=limit,
         name="render",
     )(received_next, order_second, places_second)
-    return (new_params, new_first, new_second, image)
+    return (new_params, new_first, new_second, jnp.transpose(image, (1, 0, 2)))
 
 
 def solution(mesh):

time: 117 us -> 93.1 us (0.80)
  Pallas kernels: 61.1 us -> 42 us
  local copies, waits for them, and re-layouts: 6.06 us -> 1.42 us
    pallas_call x1, Pallas kernels: 22.3 us -> 13.8 us  [shards(): pl.pallas_call(functools.partial(update_kernel, half=half), grid=(steps,)...]
    pallas_call x1, Pallas kernels: 16.8 us -> 11.3 us  [shards(): pl.pallas_call(train_kernel, out_shape=f32(32, 4, 4, LANES), in_specs=[wh...]
    unnamed x29 -> x14, local copies, waits for them, and re-layouts: 5.28 us -> 0.64 us
    pallas_call x1, Pallas kernels: 11.2 us -> 8.23 us  [shards(): pl.pallas_call(functools.partial(first_kernel, half=half), grid=(steps,),...]
    pallas_call x1, Pallas kernels: 7.49 us -> 5.3 us  [shards(): pl.pallas_call(render_kernel, out_shape=f32(3, TILE_DEV, 256), in_specs=[...]
  transfers between devices with their start and end apart: 2 -> 2, of which waited for: 2 -> 2; matrix products, arithmetic and copies ran while one was open for 1% -> 1% of each run, Pallas kernels for 3% -> 4%
where the time goes in v1:
time: 93.1 us; the launch traced here: 92.6 us
  Pallas kernels  42 us (45%)
  waiting for transfers between devices  16.7 us (18%)
  starting transfers between devices  16.1 us (17%)
  blocking collectives  15.6 us (17%)
  local copies, waits for them, and re-layouts  1.42 us (2%)
    all_to_all x2, waiting for transfers between devices, exchange(): return lax.all_to_all(flat, axis, 0, 0, tiled=True).reshape(message.shape)  16.7 us
    all_to_all x2, starting transfers between devices, exchange(): return lax.all_to_all(flat, axis, 0, 0, tiled=True).reshape(message.shape)  16.1 us
    all_to_all x1, blocking collectives, exchange(): return lax.all_to_all(flat, axis, 0, 0, tiled=True).reshape(message.shape)  15.6 us
    pallas_call x1, Pallas kernels, shards(): pl.pallas_call(functools.partial(update_kernel, half=half), grid=(steps,)...  13.8 us
    pallas_call x1, Pallas kernels, shards(): pl.pallas_call(train_kernel, out_shape=f32(32, 4, 4, LANES), in_specs=[wh...  11.3 us
    pallas_call x1, Pallas kernels, shards(): pl.pallas_call(functools.partial(first_kernel, half=half), grid=(steps,),...  8.23 us
    pallas_call x1, Pallas kernels, shards(): pl.pallas_call(render_kernel, out_shape=f32(3, TILE_DEV, 256), in_specs=[...  5.3 us
    pallas_call x1, Pallas kernels, shards(): pl.pallas_call(inverse_kernel, out_shape=(jax.ShapeDtypeStruct((32, LANES...  3.35 us
  transfers between devices with their start and end apart: 2, of which 2 were waited for; matrix products, arithmetic and copies ran while one was open for 1% of the time, Pallas kernels for 4%

profile of v1, /device:TPU:1, one launch (start us, length us, event | category | flops | bytes accessed | tf_op | source)
XLA Modules:
  0.0 92.6 jit_solution(10938221968018968818)
XLA Ops:
  0.6 0.0 copy-start
  0.6 0.0 copy-start.3
  0.7 0.0 copy-start.2
  0.7 0.0 copy-start.5
  0.7 8.2 %project_first.1 = f32[32,4,4,128]{3,2,1,0:T(4,128)} custom-call(f32[2,6]{1,0:T(2,128)} %camera_ref.3, f32[59,8192]{1,0:T(8,128)} %params_ref.3, s32[32,128]{1,0:T(8,128)} %bitcast.19), custom_call_target="tpu_custom_call" | custom-call | tf_op jit(solution)/shard_map/project_first/pallas_call | solution.py:551
  8.9 11.5 %all-to-all-start = ((f32[128,4,128]{2,1,0:T(4,128)}), f32[128,4,128]{2,1,0:T(4,128)S(1)}, u32[]{:S(2)}, u32[]{:S(2)}) async-start(f32[128,4,128]{2,1,0:T(4,128)} %bitcast.21), calls=%async_computation | async-start | bytes 524288 | tf_op jit(solution)/shard_map/all_to_all | solution.py:528
  20.4 0.0 copy-done.3
  20.4 0.1 copy.19
  20.5 0.1 reshape.49.lists_ref
  20.6 0.0 copy-done
  20.6 3.3 %inverses.1 = (s32[32,128]{1,0:T(8,128)S(1)}, s32[64,128]{1,0:T(8,128)S(1)}) custom-call(s32[32,128]{1,0:T(8,128)S(1)} %reshape.49.lists_ref, s32[32,128]{1,0:T(8,128)S(1)} %bitcast.20), custom_call_target="tpu_custom_call" | custom-call | tf_op jit(solution)/shard_map/inverses/pallas_call | solution.py:562
  24.0 0.0 copy-start.1
  24.0 0.6 copy-done.1
  24.6 0.0 copy-done.2
  24.6 0.1 reshape.50
  24.7 0.1 copy.21.targets_ref
  24.9 0.0 copy-done.5
  24.9 0.1 broadcast_in_dim_tile.6.tiles_ref
  25.0 6.2 %all-to-all-done = f32[128,4,128]{2,1,0:T(4,128)S(1)} async-done(((f32[128,4,128]{2,1,0:T(4,128)}), f32[128,4,128]{2,1,0:T(4,128)S(1)}, u32[]{:S(2)}, u32[]{:S(2)}) %all-to-all-start) | async-done | bytes 262176 | tf_op jit(solution)/shard_map/all_to_all | solution.py:528
  31.2 11.3 %train.1 = f32[32,4,4,128]{3,2,1,0:T(4,128)S(1)} custom-call(f32[32,4,4,128]{3,2,1,0:T(4,128)S(1)} %bitcast.16, s32[32,128]{1,0:T(8,128)S(1)} %reshape.49.lists_ref, s32[32,128]{1,0:T(8,128)S(1)} %get-tuple-element.10.inverse_ref, s32[1,128]{1,0:T(1,128)S(1)} %broadcast_in_dim_tile.6.tiles_ref, f32[3,64,128]{2,1,0:T(8,128)S(1)} %copy.21.targets_ref), custom_call_target="tpu_custom_call" | custom-call | tf_op jit(solution)/shard_map/train/pallas_call | solution.py:573
  42.5 15.6 %all_to_all.15 = f32[128,4,128]{2,1,0:T(4,128)} all-to-all(f32[128,4,128]{2,1,0:T(4,128)S(1)} %bitcast.18), channel_id=1, replica_groups=mesh['dev'=128] {'dev'}, dimensions={0} | all-to-all | bytes 524288 | tf_op jit(solution)/shard_map/all_to_all | solution.py:528
  58.1 0.0 copy-start.4
  58.1 0.0 copy-start.6
  58.1 13.8 %update.1 = (f32[59,8192]{1,0:T(8,128)}, f32[59,8192]{1,0:T(8,128)}, f32[59,8192]{1,0:T(8,128)}, f32[32,4,4,128]{3,2,1,0:T(4,128)}) custom-call(f32[2,6]{1,0:T(2,128)} %camera_ref.3, f32[64,128]{1,0:T(8,128)} %constant.2.clone.rates_ref, f32[32,4,4,128]{3,2,1,0:T(4,128)} %bitcast.22, s32[64,128]{1,0:T(8,128)} %copy-done.1, s32[32,128]{1,0:T(8,128)} %bitcast.26, ...), custom_call_target="tpu_custom_call" | custom-call | tf_op jit(solution)/shard_map/update/pallas_call | solution.py:586
  71.9 4.6 %all-to-all-start.2 = ((f32[128,4,128]{2,1,0:T(4,128)}), f32[128,4,128]{2,1,0:T(4,128)S(1)}, u32[]{:S(2)}, u32[]{:S(2)}) async-start(f32[128,4,128]{2,1,0:T(4,128)} %bitcast.24), calls=%async_computation.2 | async-start | bytes 524288 | tf_op jit(solution)/shard_map/all_to_all | solution.py:528
  76.5 0.0 copy-done.4
  76.6 0.1 copy.22
  76.7 0.1 reshape.57.lists_ref
  76.7 0.0 copy-done.6
  76.8 0.1 broadcast_in_dim_tile.7.tiles_ref
  76.8 10.5 %all-to-all-done.2 = f32[128,4,128]{2,1,0:T(4,128)S(1)} async-done(((f32[128,4,128]{2,1,0:T(4,128)}), f32[128,4,128]{2,1,0:T(4,128)S(1)}, u32[]{:S(2)}, u32[]{:S(2)}) %all-to-all-start.2) | async-done | bytes 262176 | tf_op jit(solution)/shard_map/all_to_all | solution.py:528
  87.3 5.3 %render.1 = f32[3,32,256]{2,1,0:T(8,128)} custom-call(f32[32,4,4,128]{3,2,1,0:T(4,128)S(1)} %bitcast.17, s32[32,128]{1,0:T(8,128)S(1)} %reshape.57.lists_ref, s32[1,128]{1,0:T(1,128)S(1)} %broadcast_in_dim_tile.7.tiles_ref), custom_call_target="tpu_custom_call" | custom-call | tf_op jit(solution)/shard_map/render/pallas_call | solution.py:604
  (3 shorter events, 0.0 us)
Async XLA Ops:
  0.6 20.0 %copy-start = (s32[1,4096]{1,0:T(1,128)S(1)}, s32[1,4096]{1,0:T(1,128)}, u32[]{:S(2)}) copy-start(s32[1,4096]{1,0:T(1,128)} %param.16) | copy-start | bytes 49156
  0.6 19.8 %copy-start.3 = (s32[32,128]{1,0:T(8,128)S(1)}, s32[32,128]{1,0:T(8,128)}, u32[]{:S(2)}) copy-start(s32[32,128]{1,0:T(8,128)} %param.18) | copy-start | bytes 49156
  0.7 23.9 %copy-start.2 = (f32[32,3,256]{2,0,1:T(8,128)S(1)}, f32[32,3,256]{2,0,1:T(8,128)}, u32[]{:S(2)}) copy-start(f32[32,3,256]{2,0,1:T(8,128)} %param.22) | copy-start | bytes 294916
  0.7 24.2 %copy-start.5 = (s32[32]{0:T(128)S(1)}, s32[32]{0:T(128)}, u32[]{:S(2)}) copy-start(s32[32]{0:T(128)} %param.20) | copy-start | bytes 388
  8.9 22.3 %all-to-all-start = ((f32[128,4,128]{2,1,0:T(4,128)}), f32[128,4,128]{2,1,0:T(4,128)S(1)}, u32[]{:S(2)}, u32[]{:S(2)}) async-start(f32[128,4,128]{2,1,0:T(4,128)} %bitcast.21), calls=%async_computation | async-start | bytes 524288 | tf_op jit(solution)/shard_map/all_to_all | solution.py:528
  24.0 0.6 copy-start.1
  58.1 18.5 %copy-start.4 = (s32[32,128]{1,0:T(8,128)S(1)}, s32[32,128]{1,0:T(8,128)}, u32[]{:S(2)}) copy-start(s32[32,128]{1,0:T(8,128)} %param.19) | copy-start | bytes 49156
  58.1 18.7 %copy-start.6 = (s32[32]{0:T(128)S(1)}, s32[32]{0:T(128)}, u32[]{:S(2)}) copy-start(s32[32]{0:T(128)} %param.21) | copy-start | bytes 388
  71.9 15.4 %all-to-all-start.2 = ((f32[128,4,128]{2,1,0:T(4,128)}), f32[128,4,128]{2,1,0:T(4,128)S(1)}, u32[]{:S(2)}, u32[]{:S(2)}) async-start(f32[128,4,128]{2,1,0:T(4,128)} %bitcast.24), calls=%async_computation.2 | async-start | bytes 524288 | tf_op jit(solution)/shard_map/all_to_all | solution.py:528

commit v2 on v1

--- a/solution.py
+++ b/solution.py
@@ -209,6 +209,10 @@
     return out
 
 
+def device_rows(g, d):
+    return pl.ds(32 * g + d, 8, stride=4)
+
+
 def pack(picked_ref, message_ref):
     nothing = jnp.zeros((8, LANES), jnp.float32)
     for g in range(4):
@@ -218,46 +222,105 @@
                 for b in range(4)
             ]
             for d, made in enumerate(block_turn(rows)):
-                message_ref[8 * g : 8 * g + 8, d, a, :] = made
-        for d in range(4):
-            message_ref[8 * g : 8 * g + 8, d, 3, :] = nothing
+                message_ref[device_rows(g, d), a, :] = made
 
 
 def unpack(message_ref, buffer_ref):
     for g in range(4):
         for a in range(3):
-            rows = [message_ref[8 * g : 8 * g + 8, d, a, :] for d in range(4)]
+            rows = [message_ref[device_rows(g, d), a, :] for d in range(4)]
             for b, made in enumerate(block_turn(rows)):
                 if 4 * a + b < 9:
                     buffer_ref[4 * a + b, 8 * g : 8 * g + 8, :] = made
 
 
-def send_splats(splats_ref, send_ref, picked_ref, message_ref):
+def greet():
+    me, devices = lax.axis_index("dev"), lax.axis_size("dev")
+    barrier = pltpu.get_barrier_semaphore()
+
+    def body(j, _):
+        pl.semaphore_signal(
+            barrier, inc=1, device_id=(lax.rem(me + j, devices),), device_id_type=pl.DeviceIdType.MESH
+        )
+        return 0
+
+    lax.fori_loop(1, devices, body, 0)
+
+
+def deliver(message_ref, landing_ref, sent, landed, meanwhile=None):
+    me, devices = lax.axis_index("dev"), lax.axis_size("dev")
+    pl.semaphore_wait(pltpu.get_barrier_semaphore(), devices - 1)
+
+    def remote(source, target, device):
+        return pltpu.make_async_remote_copy(
+            src_ref=source,
+            dst_ref=target,
+            send_sem=sent.at[0],
+            recv_sem=landed.at[0],
+            device_id=(device,),
+            device_id_type=pl.DeviceIdType.MESH,
+        )
+
+    def body(j, _):
+        other = lax.rem(me + j, devices)
+        remote(message_ref.at[other], landing_ref.at[me], other).start()
+        return 0
+
+    lax.fori_loop(1, devices, body, 0)
+    own = pltpu.make_async_copy(message_ref.at[me], landing_ref.at[me], sent.at[1])
+    own.start()
+    if meanwhile is not None:
+        meanwhile()
+    own.wait()
+    several = pl.ds(0, devices - 1)
+    remote(message_ref.at[several], landing_ref.at[several], lax.rem(me + 1, devices)).wait()
+
+
+def first_kernel(
+    camera_ref, params_ref, send_ref, lists_ref, landing_ref, from_list_ref, from_send_ref,
+    params_held, splats_ref, picked_ref, message_ref, loaded, sent, landed, *, half
+):
+    chunks = params_ref.shape[1] // CHUNK
+    loads = [
+        pltpu.make_async_copy(
+            params_ref.at[:, CHUNK * k : CHUNK * (k + 1)], params_held.at[k], loaded.at[k]
+        )
+        for k in range(chunks)
+    ]
+    for load in loads:
+        load.start()
+    greet()
+    frame = camera_frame(camera_ref, 0)
+    for k in range(chunks):
+        loads[k].wait()
+        rows = []
+        for g in range(8):
+            rows += turned([param_tile(params_held, k, g, c) for c in range(8)])
+        splats = project(rows, frame, *half)
+        for n in range(9):
+            splats_ref[n, 8 * k : 8 * k + 8, :] = splats[n]
     pick(splats_ref, send_ref, picked_ref)
     pack(picked_ref, message_ref)
 
-
-def first_kernel(
-    camera_ref, params_ref, send_ref, message_ref, splats_ref, picked_ref, frame_ref, *, half
-):
-    step = pl.program_id(0)
-
-    @pl.when(step == 0)
-    def _():
-        for n, entry in enumerate(camera_frame(camera_ref, 0)):
-            frame_ref[n] = entry
-
-    rows = []
-    for g in range(8):
-        rows += turned([params_ref[8 * g : 8 * g + 8, LANES * c : LANES * (c + 1)] for c in range(8)])
-    splats = project(rows, [frame_ref[n] for n in range(15)], *half)
-    at = pl.ds(pl.multiple_of(step * 8, 8), 8)
-    for n in range(9):
-        splats_ref[n, at, :] = splats[n]
-
-    @pl.when(step == pl.num_programs(0) - 1)
-    def _():
-        send_splats(splats_ref, send_ref, picked_ref, message_ref)
+    def meanwhile():
+        from_list_ref[...] = inverse_of(lists_ref, from_list_ref.shape[0])
+        from_send_ref[...] = inverse_of(send_ref, from_send_ref.shape[0])
+
+    deliver(message_ref, landing_ref, sent, landed, meanwhile)
+
+
+def param_tile(params_held, k, g, c):
+    at = slice(LANES * c, LANES * (c + 1))
+    if g < 7:
+        return params_held[k, 8 * g : 8 * g + 8, at]
+    return jnp.concatenate([params_held[k, 56:59, at], jnp.zeros((5, LANES), jnp.float32)], axis=0)
+
+
+def last_kernel(splats_ref, send_ref, landing_ref, picked_ref, message_ref, sent, landed):
+    greet()
+    pick(splats_ref, send_ref, picked_ref)
+    pack(picked_ref, message_ref)
+    deliver(message_ref, landing_ref, sent, landed)
 
 
 def inverse_of(ids_ref, blocks):
@@ -280,11 +343,6 @@
 
     total = lax.fori_loop(0, ids_ref.shape[0], body, jnp.zeros((2 * blocks, LANES), jnp.float32), unroll=4)
     return (total[blocks:] * 128.0 + total[:blocks]).astype(jnp.int32) - 1
-
-
-def inverse_kernel(lists_ref, send_ref, from_list_ref, from_send_ref):
-    from_list_ref[...] = inverse_of(lists_ref, from_list_ref.shape[0])
-    from_send_ref[...] = inverse_of(send_ref, from_send_ref.shape[0])
 
 
 def entry_rows(picked_ref, rows_ref):
@@ -348,10 +406,12 @@
 
 
 def train_kernel(
-    message_ref, lists_ref, inverse_ref, tiles_ref, targets_ref, back_ref,
-    buffer_ref, picked_ref, rows_ref, alpha_ref, weight_ref, sums_ref, miss_ref,
+    received_ref, lists_ref, inverse_ref, tiles_ref, targets_ref, landing_ref,
+    buffer_ref, picked_ref, rows_ref, alpha_ref, weight_ref, sums_ref, miss_ref, message_ref,
+    sent, landed,
 ):
-    unpack(message_ref, buffer_ref)
+    greet()
+    unpack(received_ref, buffer_ref)
     pick(buffer_ref, lists_ref, picked_ref)
     entry_rows(picked_ref, rows_ref)
     across, down = pixel_places(tiles_ref)
@@ -425,13 +485,14 @@
         for n in range(9):
             buffer_ref[n, 8 * g : 8 * g + 8, :] = grads[n]
     pick(buffer_ref, inverse_ref, picked_ref)
-    pack(picked_ref, back_ref)
+    pack(picked_ref, message_ref)
+    deliver(message_ref, landing_ref, sent, landed)
 
 
 def update_kernel(
-    camera_ref, rates_ref, back_ref, inverse_ref, send_ref, params_ref, first_ref, second_ref,
-    new_params_ref, new_first_ref, new_second_ref, message_ref,
-    buffer_ref, splats_ref, picked_ref, frame_ref, *, half,
+    camera_ref, rates_ref, back_ref, inverse_ref, params_ref, first_ref, second_ref,
+    new_params_ref, new_first_ref, new_second_ref, splats_ref,
+    buffer_ref, frame_ref, *, half,
 ):
     step = pl.program_id(0)
 
@@ -483,13 +544,8 @@
             fresh.append(value)
         new_rows += turned(fresh)
     splats = project(new_rows, [frame_ref[1, n] for n in range(15)], *half)
-    at = pl.ds(pl.multiple_of(step * 8, 8), 8)
     for n in range(9):
-        splats_ref[n, at, :] = splats[n]
-
-    @pl.when(step == pl.num_programs(0) - 1)
-    def _():
-        send_splats(splats_ref, send_ref, picked_ref, message_ref)
+        splats_ref[n] = splats[n]
 
 
 def render_kernel(message_ref, lists_ref, tiles_ref, image_ref, buffer_ref, picked_ref, rows_ref):
@@ -523,84 +579,85 @@
     return jax.ShapeDtypeStruct(shape, jnp.float32)
 
 
-def exchange(message, axis):
-    flat = message.reshape(-1, 4, LANES)
-    return lax.all_to_all(flat, axis, 0, 0, tiled=True).reshape(message.shape)
-
-
 def shards(
     gauss_params, adam_first, adam_second, camera, send_first, send_second,
     lists_first, lists_second, tiles_first, tiles_second, targets,
 ):
     local = gauss_params.shape[1]
-    steps = local // CHUNK
-    half = (TILES_X * 8.0, lists_first.shape[0] * lax.axis_size("dev") // TILES_X * 8.0)
-    limit = pltpu.CompilerParams(vmem_limit_bytes=48 * 1024 * 1024)
-    streamed = pltpu.CompilerParams(vmem_limit_bytes=62 * 1024 * 1024)
+    steps, blocks = local // CHUNK, local // LANES
+    devices = lax.axis_size("dev")
+    half = (TILES_X * 8.0, lists_first.shape[0] * devices // TILES_X * 8.0)
+    megabyte = 1024 * 1024
+    limit = pltpu.CompilerParams(vmem_limit_bytes=48 * megabyte)
+    streamed = pltpu.CompilerParams(vmem_limit_bytes=62 * megabyte)
+
+    def linked(number):
+        return pltpu.CompilerParams(
+            vmem_limit_bytes=60 * megabyte, collective_id=number, has_side_effects=True
+        )
+
     slots_first, slots_second = send_first.reshape(32, LANES), send_second.reshape(32, LANES)
     order_first = lists_first.T.reshape(32, LANES)
     order_second = lists_second.T.reshape(32, LANES)
     places_first = jnp.tile(tiles_first, 4)[None]
     places_second = jnp.tile(tiles_second, 4)[None]
     goals = jnp.transpose(targets.reshape(TILE_DEV, 3, 4, 64), (1, 3, 2, 0)).reshape(3, 64, LANES)
-    block = pl.BlockSpec((64, CHUNK), lambda i: (0, i))
-    fixed = pl.BlockSpec((32, LANES), lambda i: (0, 0))
-    packet = pl.BlockSpec((32, 4, 4, LANES), lambda i: (0, 0, 0, 0))
-
-
-    message = pl.pallas_call(
+    packet = (devices, 3, LANES)
+    links = [pltpu.SemaphoreType.DMA((2,)), pltpu.SemaphoreType.DMA((1,))]
+    received, from_list, from_send = pl.pallas_call(
         functools.partial(first_kernel, half=half),
-        grid=(steps,),
-        out_shape=f32(32, 4, 4, LANES),
-        in_specs=[scalars(), block, fixed],
-        out_specs=packet,
-        scratch_shapes=[vmem((9, local // LANES, LANES)), vmem((9, 32, LANES)), vmem((15, 8, LANES))],
-        compiler_params=streamed,
+        out_shape=(
+            f32(*packet),
+            jax.ShapeDtypeStruct((32, LANES), jnp.int32),
+            jax.ShapeDtypeStruct((blocks, LANES), jnp.int32),
+        ),
+        in_specs=[scalars(), pl.BlockSpec(memory_space=pl.ANY), whole(), whole()],
+        out_specs=(whole(), whole(), whole()),
+        scratch_shapes=[
+            vmem((steps, 59, CHUNK)), vmem((9, blocks, LANES)), vmem((9, 32, LANES)), vmem(packet),
+            pltpu.SemaphoreType.DMA((steps,)), *links,
+        ],
+        compiler_params=linked(1),
         name="project_first",
-    )(camera, gauss_params, slots_first)
-    received = exchange(message, "dev")
-    from_list, from_send = pl.pallas_call(
-        inverse_kernel,
-        out_shape=(
-            jax.ShapeDtypeStruct((32, LANES), jnp.int32),
-            jax.ShapeDtypeStruct((local // LANES, LANES), jnp.int32),
-        ),
-        in_specs=[whole(), whole()],
-        out_specs=(whole(), whole()),
-        compiler_params=limit,
-        name="inverses",
-    )(order_first, slots_first)
-    back = pl.pallas_call(
+    )(camera, gauss_params, slots_first, order_first)
+    returned = pl.pallas_call(
         train_kernel,
-        out_shape=f32(32, 4, 4, LANES),
+        out_shape=f32(*packet),
         in_specs=[whole()] * 5,
         out_specs=whole(),
         scratch_shapes=[
             vmem((9, 32, LANES)), vmem((9, 32, LANES)), vmem((36, 32, LANES)), vmem((32, 32, 8, LANES)),
-            vmem((32, 32, 8, LANES)), vmem((36, 32, LANES)), vmem((24, 8, LANES)),
+            vmem((32, 32, 8, LANES)), vmem((36, 32, LANES)), vmem((24, 8, LANES)), vmem(packet), *links,
         ],
-        compiler_params=limit,
+        compiler_params=linked(2),
         name="train",
     )(received, order_first, from_list, places_first, goals)
-    returned = exchange(back, "dev")
-    new_params, new_first, new_second, message_next = pl.pallas_call(
+    block = pl.BlockSpec((64, CHUNK), lambda i: (0, i))
+    new_params, new_first, new_second, splats_next = pl.pallas_call(
         functools.partial(update_kernel, half=half),
         grid=(steps,),
-        out_shape=(f32(59, local), f32(59, local), f32(59, local), f32(32, 4, 4, LANES)),
+        out_shape=(f32(59, local), f32(59, local), f32(59, local), f32(9, blocks, LANES)),
         in_specs=[
             scalars(),
             pl.BlockSpec((64, LANES), lambda i: (0, 0)),
-            packet,
+            pl.BlockSpec(packet, lambda i: (0, 0, 0)),
             pl.BlockSpec((8, LANES), lambda i: (i, 0)),
-            fixed,
             block, block, block,
         ],
-        out_specs=(block, block, block, packet),
-        scratch_shapes=[vmem((9, 32, LANES)), vmem((9, local // LANES, LANES)), vmem((9, 32, LANES)), vmem((2, 15, 8, LANES))],
+        out_specs=(block, block, block, pl.BlockSpec((9, 8, LANES), lambda i: (0, i, 0))),
+        scratch_shapes=[vmem((9, 32, LANES)), vmem((2, 15, 8, LANES))],
         compiler_params=streamed,
         name="update",
-    )(camera, jnp.asarray(rate_values()), returned, from_send, slots_second, gauss_params, adam_first, adam_second)
-    received_next = exchange(message_next, "dev")
+    )(camera, jnp.asarray(rate_values()), returned, from_send, gauss_params, adam_first, adam_second)
+    received_next = pl.pallas_call(
+        last_kernel,
+        out_shape=f32(*packet),
+        in_specs=[whole()] * 2,
+        out_specs=whole(),
+        scratch_shapes=[vmem((9, 32, LANES)), vmem(packet), *links],
+        compiler_params=linked(3),
+        name="send_next",
+    )(splats_next, slots_second)
     image = pl.pallas_call(
         render_kernel,
         out_shape=f32(3, TILE_DEV, 256),

time: 93.1 us -> 76.7 us (0.82)
  Pallas kernels: 42 us -> 71.2 us
  waiting for transfers between devices: 16.7 us -> 0 us
  starting transfers between devices: 16.1 us -> 0 us
  blocking collectives: 15.6 us -> 0 us
  local copies, waits for them, and re-layouts: 1.42 us -> 4.29 us
    pallas_call x3, Pallas kernels: 22.9 us -> 55.3 us  [the longest x1 21.4 us: shards(): pl.pallas_call(train_kernel, out_shape=f32(*packet), in_specs=[whole()] *...]
    all_to_all x2 -> x0, waiting for transfers between devices: 16.7 us -> none  [exchange(): return lax.all_to_all(flat, axis, 0, 0, tiled=True).reshape(message.shape)]
    all_to_all x2 -> x0, starting transfers between devices: 16.1 us -> none  [exchange(): return lax.all_to_all(flat, axis, 0, 0, tiled=True).reshape(message.shape)]
    all_to_all x1 -> x0, blocking collectives: 15.6 us -> none  [exchange(): return lax.all_to_all(flat, axis, 0, 0, tiled=True).reshape(message.shape)]
    pallas_call x1, Pallas kernels: 13.8 us -> 10.6 us  [shards(): pl.pallas_call(functools.partial(update_kernel, half=half), grid=(steps,)...]
  transfers between devices with their start and end apart: 2 -> 0, of which waited for: 2 -> 0; matrix products, arithmetic and copies ran while one was open for 1% -> 0% of each run, Pallas kernels for 4% -> 0%
where the time goes in v2:
time: 76.7 us; the launch traced here: 76.2 us
  Pallas kernels  71.2 us (93%)
  local copies, waits for them, and re-layouts  4.29 us (6%)
    pallas_call x1, Pallas kernels, shards(): pl.pallas_call(train_kernel, out_shape=f32(*packet), in_specs=[whole()] *...  21.4 us
    pallas_call x1, Pallas kernels, shards(): pl.pallas_call(functools.partial(first_kernel, half=half), out_shape=(f32...  19.8 us
    pallas_call x1, Pallas kernels, shards(): pl.pallas_call(last_kernel, out_shape=f32(*packet), in_specs=[whole()] *...  14.1 us
    pallas_call x1, Pallas kernels, shards(): pl.pallas_call(functools.partial(update_kernel, half=half), grid=(steps,)...  10.6 us
    pallas_call x1, Pallas kernels, shards(): pl.pallas_call(render_kernel, out_shape=f32(3, TILE_DEV, 256), in_specs=[...  5.3 us

profile of v2, /device:TPU:1, one launch (start us, length us, event | category | flops | bytes accessed | tf_op | source)
XLA Modules:
  0.0 76.2 jit_solution(2314420017220715611)
XLA Ops:
  0.6 0.0 copy-start.1
  0.6 0.0 copy-start.3
  0.7 0.9 %copy.19 = s32[128,32]{1,0:T(8,128)S(1)} copy(s32[128,32]{0,1:T(8,128)} %bitcast.13) | data formatting | bytes 32768 | tf_op jit(solution)/shard_map/transpose | solution.py:600
  1.5 0.7 reshape.29.lists_ref
  2.2 19.8 %project_first.1 = (f32[128,3,128]{2,1,0:T(4,128)}, s32[32,128]{1,0:T(8,128)}, s32[64,128]{1,0:T(8,128)}) custom-call(f32[2,6]{1,0:T(2,128)} %camera_ref.3, f32[59,8192]{1,0:T(8,128)} %params_ref.3, s32[32,128]{1,0:T(8,128)} %bitcast.12, s32[32,128]{1,0:T(8,128)} %reshape.29.lists_ref), custom_call_target="tpu_custom_call" | custom-call | tf_op jit(solution)/shard_map/project_first/pallas_call | solution.py:607
  22.0 0.0 copy-done.1
  22.0 0.1 reshape.30
  22.2 0.8 copy.21.targets_ref
  23.0 0.0 copy-done.3
  23.0 0.6 broadcast_in_dim_tile.6.tiles_ref
  23.6 21.4 %train.1.back_ref = f32[128,3,128]{2,1,0:T(4,128)} custom-call(f32[128,3,128]{2,1,0:T(4,128)} %get-tuple-element.11.received_ref, s32[32,128]{1,0:T(8,128)} %reshape.29.lists_ref, s32[32,128]{1,0:T(8,128)} %get-tuple-element.12.inverse_ref, s32[1,128]{1,0:T(1,128)} %broadcast_in_dim_tile.6.tiles_ref, f32[3,64,128]{2,1,0:T(8,128)} %copy.21.targets_ref), custom_call_target="tpu_custom_call" | custom-call | tf_op jit(solution)/shard_map/train/pallas_call | solution.py:623
  45.0 0.0 copy-start.2
  45.0 0.0 copy-start.4
  45.0 10.6 %update.1 = (f32[59,8192]{1,0:T(8,128)}, f32[59,8192]{1,0:T(8,128)}, f32[59,8192]{1,0:T(8,128)}, f32[9,64,128]{2,1,0:T(8,128)}) custom-call(f32[2,6]{1,0:T(2,128)} %camera_ref.3, f32[64,128]{1,0:T(8,128)} %constant.2.clone.rates_ref, f32[128,3,128]{2,1,0:T(4,128)} %train.1.back_ref, s32[64,128]{1,0:T(8,128)} %get-tuple-element.13.inverse_ref, ...), custom_call_target="tpu_custom_call" | custom-call | tf_op jit(solution)/shard_map/update/pallas_call | solution.py:636
  55.6 14.1 %send_next.1.message_ref = f32[128,3,128]{2,1,0:T(4,128)} custom-call(f32[9,64,128]{2,1,0:T(8,128)} %get-tuple-element.17.splats_ref, s32[32,128]{1,0:T(8,128)} %bitcast.14), custom_call_target="tpu_custom_call" | custom-call | tf_op jit(solution)/shard_map/send_next/pallas_call | solution.py:652
  69.7 0.0 copy-done.2
  69.7 0.1 copy.22
  69.8 0.1 reshape.33.lists_ref
  69.9 0.0 copy-done.4
  69.9 0.1 broadcast_in_dim_tile.7.tiles_ref
  70.0 0.0 copy-start
  70.0 0.9 %copy-done = f32[128,3,128]{2,1,0:T(4,128)S(1)} copy-done((f32[128,3,128]{2,1,0:T(4,128)S(1)}, f32[128,3,128]{2,1,0:T(4,128)}, u32[]{:S(2)}) %copy-start) | copy-done | bytes 196632
  70.9 5.3 %render.1 = f32[3,32,256]{2,1,0:T(8,128)} custom-call(f32[128,3,128]{2,1,0:T(4,128)S(1)} %copy-done, s32[32,128]{1,0:T(8,128)S(1)} %reshape.33.lists_ref, s32[1,128]{1,0:T(1,128)S(1)} %broadcast_in_dim_tile.7.tiles_ref), custom_call_target="tpu_custom_call" | custom-call | tf_op jit(solution)/shard_map/render/pallas_call | solution.py:661
  (3 shorter events, 0.0 us)
Async XLA Ops:
  0.6 21.4 %copy-start.1 = (f32[32,3,256]{2,0,1:T(8,128)S(1)}, f32[32,3,256]{2,0,1:T(8,128)}, u32[]{:S(2)}) copy-start(f32[32,3,256]{2,0,1:T(8,128)} %param.22) | copy-start | bytes 294916
  0.6 22.3 %copy-start.3 = (s32[32]{0:T(128)S(1)}, s32[32]{0:T(128)}, u32[]{:S(2)}) copy-start(s32[32]{0:T(128)} %param.20) | copy-start | bytes 388
  45.0 24.7 %copy-start.2 = (s32[32,128]{1,0:T(8,128)S(1)}, s32[32,128]{1,0:T(8,128)}, u32[]{:S(2)}) copy-start(s32[32,128]{1,0:T(8,128)} %param.19) | copy-start | bytes 49156
  45.0 24.9 %copy-start.4 = (s32[32]{0:T(128)S(1)}, s32[32]{0:T(128)}, u32[]{:S(2)}) copy-start(s32[32]{0:T(128)} %param.21) | copy-start | bytes 388
  70.0 1.0 %copy-start = (f32[128,3,128]{2,1,0:T(4,128)S(1)}, f32[128,3,128]{2,1,0:T(4,128)}, u32[]{:S(2)}) copy-start(f32[128,3,128]{2,1,0:T(4,128)} %send_next.1.message_ref) | copy-start | bytes 589828

commit v3 on v2

--- a/solution.py
+++ b/solution.py
@@ -52,13 +52,22 @@
     return np.broadcast_to(values[:, None], (64, LANES)).astype(np.float32)
 
 
+def small_turn(angle):
+    square = angle * angle
+    cosine = 1.0 + square * (
+        -1 / 2 + square * (1 / 24 + square * (-1 / 720 + square * (1 / 40320 - square / 3628800)))
+    )
+    sine = angle * (
+        1.0 + square * (-1 / 6 + square * (1 / 120 + square * (-1 / 5040 + square / 362880)))
+    )
+    return cosine, sine
+
+
 def camera_frame(camera_ref, view):
     def full(k):
         return jnp.full((8, LANES), camera_ref[view, k], jnp.float32)
 
-    ca, sa = jnp.cos(full(0)), jnp.sin(full(0))
-    cb, sb = jnp.cos(full(1)), jnp.sin(full(1))
-    cc, sc = jnp.cos(full(2)), jnp.sin(full(2))
+    (ca, sa), (cb, sb), (cc, sc) = [small_turn(full(k)) for k in range(3)]
     rot = [
         [cc * cb, cc * (sb * sa) - sc * ca, cc * (sb * ca) + sc * sa],
         [sc * cb, sc * (sb * sa) + cc * ca, sc * (sb * ca) - cc * sa],
@@ -247,9 +256,12 @@
     lax.fori_loop(1, devices, body, 0)
 
 
+def greeted():
+    pl.semaphore_wait(pltpu.get_barrier_semaphore(), lax.axis_size("dev") - 1)
+
+
 def deliver(message_ref, landing_ref, sent, landed, meanwhile=None):
     me, devices = lax.axis_index("dev"), lax.axis_size("dev")
-    pl.semaphore_wait(pltpu.get_barrier_semaphore(), devices - 1)
 
     def remote(source, target, device):
         return pltpu.make_async_remote_copy(
@@ -276,10 +288,7 @@
     remote(message_ref.at[several], landing_ref.at[several], lax.rem(me + 1, devices)).wait()
 
 
-def first_kernel(
-    camera_ref, params_ref, send_ref, lists_ref, landing_ref, from_list_ref, from_send_ref,
-    params_held, splats_ref, picked_ref, message_ref, loaded, sent, landed, *, half
-):
+def project_all(view, camera_ref, params_ref, params_held, splats_ref, loaded, half):
     chunks = params_ref.shape[1] // CHUNK
     loads = [
         pltpu.make_async_copy(
@@ -290,7 +299,7 @@
     for load in loads:
         load.start()
     greet()
-    frame = camera_frame(camera_ref, 0)
+    frame = camera_frame(camera_ref, view)
     for k in range(chunks):
         loads[k].wait()
         rows = []
@@ -299,14 +308,6 @@
         splats = project(rows, frame, *half)
         for n in range(9):
             splats_ref[n, 8 * k : 8 * k + 8, :] = splats[n]
-    pick(splats_ref, send_ref, picked_ref)
-    pack(picked_ref, message_ref)
-
-    def meanwhile():
-        from_list_ref[...] = inverse_of(lists_ref, from_list_ref.shape[0])
-        from_send_ref[...] = inverse_of(send_ref, from_send_ref.shape[0])
-
-    deliver(message_ref, landing_ref, sent, landed, meanwhile)
 
 
 def param_tile(params_held, k, g, c):
@@ -316,11 +317,23 @@
     return jnp.concatenate([params_held[k, 56:59, at], jnp.zeros((5, LANES), jnp.float32)], axis=0)
 
 
-def last_kernel(splats_ref, send_ref, landing_ref, picked_ref, message_ref, sent, landed):
-    greet()
-    pick(splats_ref, send_ref, picked_ref)
-    pack(picked_ref, message_ref)
-    deliver(message_ref, landing_ref, sent, landed)
+def list_order(lists_ref, turn_ref, order_ref):
+    turn_ref[...] = jnp.transpose(jnp.concatenate([lists_ref[...]] * 4, axis=0))
+    block = lax.broadcasted_iota(jnp.int32, (32, LANES), 1) >> 5
+    made = None
+    for part in range(4):
+        value = turn_ref[pl.ds(part, 32, stride=4), :]
+        made = value if made is None else jnp.where(block == part, value, made)
+    order_ref[...] = made
+
+
+def goal_order(targets_ref, goals_ref):
+    for c in range(3):
+        left, right = targets_ref[c, :, 0:128], targets_ref[c, :, 128:256]
+        stacked = jnp.concatenate(
+            [left, pltpu.roll(left, 64, 1), right, pltpu.roll(right, 64, 1)], axis=0
+        )
+        goals_ref[c] = jnp.transpose(stacked)[0:64, :]
 
 
 def inverse_of(ids_ref, blocks):
@@ -364,7 +377,7 @@
 def pixel_places(tiles_ref):
     lane = lax.broadcasted_iota(jnp.int32, (8, LANES), 1)
     sub = lax.broadcasted_iota(jnp.int32, (8, LANES), 0)
-    tiles = jnp.broadcast_to(tiles_ref[0:1, :], (8, LANES))
+    tiles = jnp.broadcast_to(jnp.concatenate([tiles_ref[...]] * 4, axis=1), (8, LANES))
     column = (tiles & (TILES_X - 1)) * 16 + sub
     row = (tiles >> 7) * 16 + (lane >> 5) * 4
     across = [column.astype(jnp.float32) + (0.5 + 8 * p) for p in range(2)]
@@ -406,19 +419,30 @@
 
 
 def train_kernel(
-    received_ref, lists_ref, inverse_ref, tiles_ref, targets_ref, landing_ref,
-    buffer_ref, picked_ref, rows_ref, alpha_ref, weight_ref, sums_ref, miss_ref, message_ref,
-    sent, landed,
+    camera_ref, params_ref, send_ref, lists_ref, tiles_ref, targets_ref, returned_ref, from_send_ref,
+    params_held, splats_ref, buffer_ref, picked_ref, rows_ref, alpha_ref, weight_ref, sums_ref,
+    miss_ref, message_ref, landing_ref, turn_ref, order_ref, from_list_ref, goals_ref,
+    loaded, sent, landed, sent_back, landed_back, *, half,
 ):
-    greet()
-    unpack(received_ref, buffer_ref)
-    pick(buffer_ref, lists_ref, picked_ref)
+    project_all(0, camera_ref, params_ref, params_held, splats_ref, loaded, half)
+    pick(splats_ref, send_ref, picked_ref)
+    pack(picked_ref, message_ref.at[0])
+    greeted()
+
+    def before_landing():
+        list_order(lists_ref, turn_ref, order_ref)
+        goal_order(targets_ref, goals_ref)
+        from_list_ref[...] = inverse_of(order_ref, 32)
+
+    deliver(message_ref.at[0], landing_ref, sent, landed, before_landing)
+    unpack(landing_ref, buffer_ref)
+    pick(buffer_ref, order_ref, picked_ref)
     entry_rows(picked_ref, rows_ref)
     across, down = pixel_places(tiles_ref)
     light = composite(rows_ref, across, down, (alpha_ref, weight_ref))
     for c in range(3):
         for v in range(8):
-            miss_ref[8 * c + v] = light[c][v] - targets_ref[c, 8 * v : 8 * v + 8, :]
+            miss_ref[8 * c + v] = light[c][v] - goals_ref[c, 8 * v : 8 * v + 8, :]
 
     def body(step, behind):
         j = LIST_LEN // 4 - 1 - step
@@ -484,14 +508,18 @@
         ]
         for n in range(9):
             buffer_ref[n, 8 * g : 8 * g + 8, :] = grads[n]
-    pick(buffer_ref, inverse_ref, picked_ref)
-    pack(picked_ref, message_ref)
-    deliver(message_ref, landing_ref, sent, landed)
+    pick(buffer_ref, from_list_ref, picked_ref)
+    pack(picked_ref, message_ref.at[1])
+
+    def before_return():
+        from_send_ref[...] = inverse_of(send_ref, from_send_ref.shape[0])
+
+    deliver(message_ref.at[1], returned_ref, sent_back, landed_back, before_return)
 
 
 def update_kernel(
     camera_ref, rates_ref, back_ref, inverse_ref, params_ref, first_ref, second_ref,
-    new_params_ref, new_first_ref, new_second_ref, splats_ref,
+    new_params_ref, new_first_ref, new_second_ref,
     buffer_ref, frame_ref, *, half,
 ):
     step = pl.program_id(0)
@@ -499,15 +527,14 @@
     @pl.when(step == 0)
     def _():
         unpack(back_ref, buffer_ref)
-        for view in range(2):
-            for n, entry in enumerate(camera_frame(camera_ref, view)):
-                frame_ref[view, n] = entry
+        for n, entry in enumerate(camera_frame(camera_ref, 0)):
+            frame_ref[n] = entry
 
     slot_grads = pick_eight(buffer_ref, inverse_ref[...])
     rows = []
     for g in range(8):
         rows += turned([params_ref[8 * g : 8 * g + 8, LANES * c : LANES * (c + 1)] for c in range(8)])
-    frame = [frame_ref[0, n] for n in range(15)]
+    frame = [frame_ref[n] for n in range(15)]
     used = rows[:10] + [None] + rows[11:59]
 
     def view_first(*leaves):
@@ -525,11 +552,9 @@
     grads = list(pullback((slot_grads[0], slot_grads[1], *cover_grads, *slot_grads[6:])))
     opacity_grad = slot_grads[5] * (1.0 - jax.nn.sigmoid(rows[10]))
     grads = grads[:10] + [opacity_grad] + grads[10:] + [jnp.zeros((8, LANES), jnp.float32)] * 5
-    new_rows = []
     for g in range(8):
         columns = turned(grads[8 * g : 8 * g + 8])
         rate = rates_ref[8 * g : 8 * g + 8, :]
-        fresh = []
         for c in range(8):
             at = (slice(8 * g, 8 * g + 8), slice(LANES * c, LANES * (c + 1)))
             gradient = columns[c]
@@ -541,16 +566,22 @@
             new_first_ref[at] = first
             new_second_ref[at] = second
             new_params_ref[at] = value
-            fresh.append(value)
-        new_rows += turned(fresh)
-    splats = project(new_rows, [frame_ref[1, n] for n in range(15)], *half)
-    for n in range(9):
-        splats_ref[n] = splats[n]
-
-
-def render_kernel(message_ref, lists_ref, tiles_ref, image_ref, buffer_ref, picked_ref, rows_ref):
-    unpack(message_ref, buffer_ref)
-    pick(buffer_ref, lists_ref, picked_ref)
+
+
+def render_kernel(
+    camera_ref, params_ref, send_ref, lists_ref, tiles_ref, image_ref,
+    params_held, splats_ref, buffer_ref, picked_ref, rows_ref, message_ref, landing_ref,
+    turn_ref, order_ref, loaded, sent, landed, *, half,
+):
+    project_all(1, camera_ref, params_ref, params_held, splats_ref, loaded, half)
+    pick(splats_ref, send_ref, picked_ref)
+    pack(picked_ref, message_ref)
+    greeted()
+    deliver(
+        message_ref, landing_ref, sent, landed, lambda: list_order(lists_ref, turn_ref, order_ref)
+    )
+    unpack(landing_ref, buffer_ref)
+    pick(buffer_ref, order_ref, picked_ref)
     entry_rows(picked_ref, rows_ref)
     across, down = pixel_places(tiles_ref)
     light = composite(rows_ref, across, down, None)
@@ -588,7 +619,6 @@
     devices = lax.axis_size("dev")
     half = (TILES_X * 8.0, lists_first.shape[0] * devices // TILES_X * 8.0)
     megabyte = 1024 * 1024
-    limit = pltpu.CompilerParams(vmem_limit_bytes=48 * megabyte)
     streamed = pltpu.CompilerParams(vmem_limit_bytes=62 * megabyte)
 
     def linked(number):
@@ -597,46 +627,34 @@
         )
 
     slots_first, slots_second = send_first.reshape(32, LANES), send_second.reshape(32, LANES)
-    order_first = lists_first.T.reshape(32, LANES)
-    order_second = lists_second.T.reshape(32, LANES)
-    places_first = jnp.tile(tiles_first, 4)[None]
-    places_second = jnp.tile(tiles_second, 4)[None]
-    goals = jnp.transpose(targets.reshape(TILE_DEV, 3, 4, 64), (1, 3, 2, 0)).reshape(3, 64, LANES)
     packet = (devices, 3, LANES)
     links = [pltpu.SemaphoreType.DMA((2,)), pltpu.SemaphoreType.DMA((1,))]
-    received, from_list, from_send = pl.pallas_call(
-        functools.partial(first_kernel, half=half),
-        out_shape=(
-            f32(*packet),
-            jax.ShapeDtypeStruct((32, LANES), jnp.int32),
-            jax.ShapeDtypeStruct((blocks, LANES), jnp.int32),
-        ),
-        in_specs=[scalars(), pl.BlockSpec(memory_space=pl.ANY), whole(), whole()],
-        out_specs=(whole(), whole(), whole()),
+    loading = pltpu.SemaphoreType.DMA((steps,))
+    held = [vmem((steps, 59, CHUNK)), vmem((9, blocks, LANES)), vmem((9, 32, LANES)), vmem((9, 32, LANES))]
+    anywhere = pl.BlockSpec(memory_space=pl.ANY)
+
+    def integers(*shape):
+        return pltpu.VMEM(shape, jnp.int32)
+
+    returned, from_send = pl.pallas_call(
+        functools.partial(train_kernel, half=half),
+        out_shape=(f32(*packet), jax.ShapeDtypeStruct((blocks, LANES), jnp.int32)),
+        in_specs=[scalars(), anywhere, whole(), whole(), whole(), whole()],
+        out_specs=(whole(), whole()),
         scratch_shapes=[
-            vmem((steps, 59, CHUNK)), vmem((9, blocks, LANES)), vmem((9, 32, LANES)), vmem(packet),
-            pltpu.SemaphoreType.DMA((steps,)), *links,
+            *held, vmem((36, 32, LANES)), vmem((32, 32, 8, LANES)), vmem((32, 32, 8, LANES)),
+            vmem((36, 32, LANES)), vmem((24, 8, LANES)), vmem((2, *packet)), vmem(packet),
+            integers(LANES, LANES), integers(32, LANES), integers(32, LANES), vmem((3, 64, LANES)),
+            loading, *links, *links,
         ],
         compiler_params=linked(1),
-        name="project_first",
-    )(camera, gauss_params, slots_first, order_first)
-    returned = pl.pallas_call(
-        train_kernel,
-        out_shape=f32(*packet),
-        in_specs=[whole()] * 5,
-        out_specs=whole(),
-        scratch_shapes=[
-            vmem((9, 32, LANES)), vmem((9, 32, LANES)), vmem((36, 32, LANES)), vmem((32, 32, 8, LANES)),
-            vmem((32, 32, 8, LANES)), vmem((36, 32, LANES)), vmem((24, 8, LANES)), vmem(packet), *links,
-        ],
-        compiler_params=linked(2),
         name="train",
-    )(received, order_first, from_list, places_first, goals)
+    )(camera, gauss_params, slots_first, lists_first, tiles_first[None], jnp.transpose(targets, (1, 0, 2)))
     block = pl.BlockSpec((64, CHUNK), lambda i: (0, i))
-    new_params, new_first, new_second, splats_next = pl.pallas_call(
+    new_params, new_first, new_second = pl.pallas_call(
         functools.partial(update_kernel, half=half),
         grid=(steps,),
-        out_shape=(f32(59, local), f32(59, local), f32(59, local), f32(9, blocks, LANES)),
+        out_shape=(f32(59, local), f32(59, local), f32(59, local)),
         in_specs=[
             scalars(),
             pl.BlockSpec((64, LANES), lambda i: (0, 0)),
@@ -644,29 +662,23 @@
             pl.BlockSpec((8, LANES), lambda i: (i, 0)),
             block, block, block,
         ],
-        out_specs=(block, block, block, pl.BlockSpec((9, 8, LANES), lambda i: (0, i, 0))),
-        scratch_shapes=[vmem((9, 32, LANES)), vmem((2, 15, 8, LANES))],
+        out_specs=(block, block, block),
+        scratch_shapes=[vmem((9, 32, LANES)), vmem((15, 8, LANES))],
         compiler_params=streamed,
         name="update",
     )(camera, jnp.asarray(rate_values()), returned, from_send, gauss_params, adam_first, adam_second)
-    received_next = pl.pallas_call(
-        last_kernel,
-        out_shape=f32(*packet),
-        in_specs=[whole()] * 2,
+    image = pl.pallas_call(
+        functools.partial(render_kernel, half=half),
+        out_shape=f32(3, TILE_DEV, 256),
+        in_specs=[scalars(), anywhere, whole(), whole(), whole()],
         out_specs=whole(),
-        scratch_shapes=[vmem((9, 32, LANES)), vmem(packet), *links],
-        compiler_params=linked(3),
-        name="send_next",
-    )(splats_next, slots_second)
-    image = pl.pallas_call(
-        render_kernel,
-        out_shape=f32(3, TILE_DEV, 256),
-        in_specs=[whole()] * 3,
-        out_specs=whole(),
-        scratch_shapes=[vmem((9, 32, LANES)), vmem((9, 32, LANES)), vmem((36, 32, LANES))],
-        compiler_params=limit,
+        scratch_shapes=[
+            *held, vmem((36, 32, LANES)), vmem(packet), vmem(packet),
+            integers(LANES, LANES), integers(32, LANES), loading, *links,
+        ],
+        compiler_params=linked(2),
         name="render",
-    )(received_next, order_second, places_second)
+    )(camera, new_params, slots_second, lists_second, tiles_second[None])
     return (new_params, new_first, new_second, jnp.transpose(image, (1, 0, 2)))
 
 

time: 76.7 us -> 70.5 us (0.919)
  Pallas kernels: 71.2 us -> 67.9 us
  local copies, waits for them, and re-layouts: 4.29 us -> 1.54 us
    pallas_call x4 -> x2, Pallas kernels: 60.6 us -> 57.8 us  [the longest x1 38.2 us: shards(): pl.pallas_call(functools.partial(train_kernel, half=half), out_shape=(f32...]
    reshape x5 -> x0, local copies, waits for them, and re-layouts: 1.67 us -> none  [the longest x1 0.76 us: shards(): jnp.transpose(targets.reshape(TILE_DEV, 3, 4, 64), (1, 3, 2, 0))]
    transpose x2 -> x0, local copies, waits for them, and re-layouts: 0.95 us -> none  [the longest x1 0.86 us: shards(): order_first = lists_first.T.reshape(32, LANES)]
    unnamed x10 -> x1, local copies, waits for them, and re-layouts: 0.97 us -> 1.54 us
where the time goes in v3:
time: 70.5 us; the launch traced here: 70.1 us
  Pallas kernels  67.9 us (96%)
  local copies, waits for them, and re-layouts  1.54 us (2%)
    pallas_call x1, Pallas kernels, shards(): pl.pallas_call(functools.partial(train_kernel, half=half), out_shape=(f32...  38.2 us
    pallas_call x1, Pallas kernels, shards(): pl.pallas_call(functools.partial(render_kernel, half=half), out_shape=f32...  19.6 us
    pallas_call x1, Pallas kernels, shards(): pl.pallas_call(functools.partial(update_kernel, half=half), grid=(steps,)...  10.1 us
    unnamed x1, local copies, waits for them, and re-layouts  1.54 us

profile of v3, /device:TPU:1, one launch (start us, length us, event | category | flops | bytes accessed | tf_op | source)
XLA Modules:
  0.0 70.1 jit_solution(17449530696153618569)
XLA Ops:
  0.6 38.2 %train.1 = (f32[128,3,128]{2,1,0:T(4,128)}, s32[64,128]{1,0:T(8,128)}) custom-call(f32[2,6]{1,0:T(2,128)} %camera_ref.5, f32[59,8192]{1,0:T(8,128)} %params_ref.3, s32[32,128]{1,0:T(8,128)} %bitcast.8, s32[32,128]{1,0:T(8,128)} %lists_ref.2, s32[1,32]{1,0:T(1,128)} %bitcast.10, f32[3,32,256]{2,1,0:T(8,128)} %bitcast.7), custom_call_target="tpu_custom_call" | custom-call | tf_op jit(solution)/shard_map/train/pallas_call | solution.py:639
  38.8 10.1 %update.1 = (f32[59,8192]{1,0:T(8,128)}, f32[59,8192]{1,0:T(8,128)}, f32[59,8192]{1,0:T(8,128)}) custom-call(f32[2,6]{1,0:T(2,128)} %camera_ref.5, f32[64,128]{1,0:T(8,128)} %constant.2.clone.rates_ref, f32[128,3,128]{2,1,0:T(4,128)} %get-tuple-element.9.back_ref, s32[64,128]{1,0:T(8,128)} %get-tuple-element.10.inverse_ref, f32[59,8192]{1,0:T(8,128)} %params_ref.3, ...), custom_call_target="tpu_custom_call" | custom-call | tf_op jit(solution)/shard_map/update/pallas_call | solution.py:654
  48.9 19.6 %render.1 = f32[3,32,256]{2,1,0:T(8,128)} custom-call(f32[2,6]{1,0:T(2,128)} %camera_ref.5, f32[59,8192]{1,0:T(8,128)} %get-tuple-element.18.params_ref, s32[32,128]{1,0:T(8,128)} %bitcast.9, s32[32,128]{1,0:T(8,128)} %lists_ref.3, s32[1,32]{1,0:T(1,128)} %bitcast.11), custom_call_target="tpu_custom_call" | custom-call | tf_op jit(solution)/shard_map/render/pallas_call | solution.py:670
  68.5 1.5 %copy.17 = f32[32,3,256]{2,0,1:T(8,128)} copy(f32[32,3,256]{2,0,1:T(8,128)} %bitcast.6) | data formatting | bytes 196608

commit v4 on v3

--- a/solution.py
+++ b/solution.py
@@ -222,16 +222,12 @@
     return pl.ds(32 * g + d, 8, stride=4)
 
 
-def pack(picked_ref, message_ref):
+def pack_group(values, message_ref, g):
     nothing = jnp.zeros((8, LANES), jnp.float32)
-    for g in range(4):
-        for a in range(3):
-            rows = [
-                picked_ref[4 * a + b, 8 * g : 8 * g + 8, :] if 4 * a + b < 9 else nothing
-                for b in range(4)
-            ]
-            for d, made in enumerate(block_turn(rows)):
-                message_ref[device_rows(g, d), a, :] = made
+    for a in range(3):
+        rows = [values[4 * a + b] if 4 * a + b < 9 else nothing for b in range(4)]
+        for d, made in enumerate(block_turn(rows)):
+            message_ref[device_rows(g, d), a, :] = made
 
 
 def unpack(message_ref, buffer_ref):
@@ -260,8 +256,12 @@
     pl.semaphore_wait(pltpu.get_barrier_semaphore(), lax.axis_size("dev") - 1)
 
 
-def deliver(message_ref, landing_ref, sent, landed, meanwhile=None):
+def deliver(
+    source_ref, wanted_ref, message_ref, landing_ref, sent, landed, ready, meanwhile
+):
     me, devices = lax.axis_index("dev"), lax.axis_size("dev")
+    share = devices // 4
+    home, place = lax.div(me, share), lax.rem(me, share)
 
     def remote(source, target, device):
         return pltpu.make_async_remote_copy(
@@ -273,16 +273,25 @@
             device_id_type=pl.DeviceIdType.MESH,
         )
 
-    def body(j, _):
-        other = lax.rem(me + j, devices)
-        remote(message_ref.at[other], landing_ref.at[me], other).start()
-        return 0
-
-    lax.fori_loop(1, devices, body, 0)
+    for ahead in (2, 1, 3, 0):
+        g = lax.rem(home + ahead, 4)
+        at = pl.ds(pl.multiple_of(g * 8, 8), 8)
+        pack_group(pick_eight(source_ref, wanted_ref[at, :]), message_ref, g)
+        if ahead == 2 and ready is not None:
+            ready()
+
+        def body(i, _):
+            other = g * share + lax.rem(place + i, share)
+            remote(message_ref.at[other], landing_ref.at[me], other).start()
+            return 0
+
+        if ahead:
+            lax.fori_loop(share // 2, share + share // 2, body, 0)
+        else:
+            lax.fori_loop(1, share, body, 0)
     own = pltpu.make_async_copy(message_ref.at[me], landing_ref.at[me], sent.at[1])
     own.start()
-    if meanwhile is not None:
-        meanwhile()
+    meanwhile()
     own.wait()
     several = pl.ds(0, devices - 1)
     remote(message_ref.at[several], landing_ref.at[several], lax.rem(me + 1, devices)).wait()
@@ -425,16 +434,14 @@
     loaded, sent, landed, sent_back, landed_back, *, half,
 ):
     project_all(0, camera_ref, params_ref, params_held, splats_ref, loaded, half)
-    pick(splats_ref, send_ref, picked_ref)
-    pack(picked_ref, message_ref.at[0])
-    greeted()
-
     def before_landing():
         list_order(lists_ref, turn_ref, order_ref)
         goal_order(targets_ref, goals_ref)
         from_list_ref[...] = inverse_of(order_ref, 32)
 
-    deliver(message_ref.at[0], landing_ref, sent, landed, before_landing)
+    deliver(
+        splats_ref, send_ref, message_ref.at[0], landing_ref, sent, landed, greeted, before_landing
+    )
     unpack(landing_ref, buffer_ref)
     pick(buffer_ref, order_ref, picked_ref)
     entry_rows(picked_ref, rows_ref)
@@ -508,13 +515,14 @@
         ]
         for n in range(9):
             buffer_ref[n, 8 * g : 8 * g + 8, :] = grads[n]
-    pick(buffer_ref, from_list_ref, picked_ref)
-    pack(picked_ref, message_ref.at[1])
 
     def before_return():
         from_send_ref[...] = inverse_of(send_ref, from_send_ref.shape[0])
 
-    deliver(message_ref.at[1], returned_ref, sent_back, landed_back, before_return)
+    deliver(
+        buffer_ref, from_list_ref, message_ref.at[1], returned_ref, sent_back, landed_back,
+        None, before_return,
+    )
 
 
 def update_kernel(
@@ -574,11 +582,9 @@
     turn_ref, order_ref, loaded, sent, landed, *, half,
 ):
     project_all(1, camera_ref, params_ref, params_held, splats_ref, loaded, half)
-    pick(splats_ref, send_ref, picked_ref)
-    pack(picked_ref, message_ref)
-    greeted()
     deliver(
-        message_ref, landing_ref, sent, landed, lambda: list_order(lists_ref, turn_ref, order_ref)
+        splats_ref, send_ref, message_ref, landing_ref, sent, landed, greeted,
+        lambda: list_order(lists_ref, turn_ref, order_ref),
     )
     unpack(landing_ref, buffer_ref)
     pick(buffer_ref, order_ref, picked_ref)
@@ -623,7 +629,9 @@
 
     def linked(number):
         return pltpu.CompilerParams(
-            vmem_limit_bytes=60 * megabyte, collective_id=number, has_side_effects=True
+            vmem_limit_bytes=(60 if number == 1 else 52) * megabyte,
+            collective_id=number,
+            has_side_effects=True,
         )
 
     slots_first, slots_second = send_first.reshape(32, LANES), send_second.reshape(32, LANES)
@@ -631,7 +639,7 @@
     links = [pltpu.SemaphoreType.DMA((2,)), pltpu.SemaphoreType.DMA((1,))]
     loading = pltpu.SemaphoreType.DMA((steps,))
     held = [vmem((steps, 59, CHUNK)), vmem((9, blocks, LANES)), vmem((9, 32, LANES)), vmem((9, 32, LANES))]
-    anywhere = pl.BlockSpec(memory_space=pl.ANY)
+    outside = pl.BlockSpec(memory_space=pltpu.HBM)
 
     def integers(*shape):
         return pltpu.VMEM(shape, jnp.int32)
@@ -639,7 +647,7 @@
     returned, from_send = pl.pallas_call(
         functools.partial(train_kernel, half=half),
         out_shape=(f32(*packet), jax.ShapeDtypeStruct((blocks, LANES), jnp.int32)),
-        in_specs=[scalars(), anywhere, whole(), whole(), whole(), whole()],
+        in_specs=[scalars(), outside, whole(), whole(), whole(), whole()],
         out_specs=(whole(), whole()),
         scratch_shapes=[
             *held, vmem((36, 32, LANES)), vmem((32, 32, 8, LANES)), vmem((32, 32, 8, LANES)),
@@ -670,7 +678,7 @@
     image = pl.pallas_call(
         functools.partial(render_kernel, half=half),
         out_shape=f32(3, TILE_DEV, 256),
-        in_specs=[scalars(), anywhere, whole(), whole(), whole()],
+        in_specs=[scalars(), outside, whole(), whole(), whole()],
         out_specs=whole(),
         scratch_shapes=[
             *held, vmem((36, 32, LANES)), vmem(packet), vmem(packet),

time: 70.5 us -> 69.1 us (0.980)
  local copies, waits for them, and re-layouts: 1.54 us -> 0.67 us
    unnamed x1 -> x9, local copies, waits for them, and re-layouts: 1.54 us -> 0.67 us
where the time goes in v4:
time: 69.1 us; the launch traced here: 68.8 us
  Pallas kernels  67.4 us (98%)
  between operations  0.71 us (1%)
    pallas_call x1, Pallas kernels, shards(): pl.pallas_call(functools.partial(train_kernel, half=half), out_shape=(f32...  38.3 us
    pallas_call x1, Pallas kernels, shards(): pl.pallas_call(functools.partial(render_kernel, half=half), out_shape=f32...  19.1 us
    pallas_call x1, Pallas kernels, shards(): pl.pallas_call(functools.partial(update_kernel, half=half), grid=(steps,)...  10.1 us

profile of v4, /device:TPU:1, one launch (start us, length us, event | category | flops | bytes accessed | tf_op | source)
XLA Modules:
  0.0 68.8 jit_solution(13161838234964748923)
XLA Ops:
  0.6 38.3 %train.1 = (f32[128,3,128]{2,1,0:T(4,128)}, s32[64,128]{1,0:T(8,128)}) custom-call(f32[2,6]{1,0:T(2,128)} %camera_ref.5, f32[59,8192]{1,0:T(8,128)} %params_ref.3, s32[32,128]{1,0:T(8,128)} %bitcast.10, s32[32,128]{1,0:T(8,128)} %lists_ref.2, s32[1,32]{1,0:T(1,128)} %bitcast.11, f32[3,32,256]{2,1,0:T(8,128)} %bitcast.9), custom_call_target="tpu_custom_call" | custom-call | tf_op jit(solution)/shard_map/train/pallas_call | solution.py:647
  38.9 0.0 copy-start
  38.9 0.0 copy-start.1
  38.9 0.0 copy-start.2
  38.9 0.0 copy-start.3
  39.0 10.1 %update.1 = (f32[59,8192]{1,0:T(8,128)}, f32[59,8192]{1,0:T(8,128)}, f32[59,8192]{1,0:T(8,128)}) custom-call(f32[2,6]{1,0:T(2,128)} %camera_ref.5, f32[64,128]{1,0:T(8,128)} %constant.2.clone.rates_ref, f32[128,3,128]{2,1,0:T(4,128)} %get-tuple-element.9.back_ref, s32[64,128]{1,0:T(8,128)} %get-tuple-element.10.inverse_ref, f32[59,8192]{1,0:T(8,128)} %params_ref.3, ...), custom_call_target="tpu_custom_call" | custom-call | tf_op jit(solution)/shard_map/update/pallas_call | solution.py:662
  49.0 0.0 copy-done
  49.1 0.0 copy-done.1
  49.1 0.0 copy-done.2
  49.1 0.0 copy-done.3
  49.1 19.1 %render.1 = f32[3,32,256]{2,1,0:T(8,128)S(1)} custom-call(f32[2,6]{1,0:T(2,128)S(1)} %copy-done.2, f32[59,8192]{1,0:T(8,128)} %get-tuple-element.18.params_ref, s32[32,128]{1,0:T(8,128)S(1)} %bitcast.7, s32[32,128]{1,0:T(8,128)S(1)} %copy-done.1, s32[1,32]{1,0:T(1,128)S(1)} %bitcast.8), custom_call_target="tpu_custom_call" | custom-call | tf_op jit(solution)/shard_map/render/pallas_call | solution.py:678
  68.2 0.6 copy.17
Async XLA Ops:
  38.9 10.1 %copy-start = (s32[1,4096]{1,0:T(1,128)S(1)}, s32[1,4096]{1,0:T(1,128)}, u32[]{:S(2)}) copy-start(s32[1,4096]{1,0:T(1,128)} %param.17) | copy-start | bytes 49156
  38.9 10.1 %copy-start.1 = (s32[32,128]{1,0:T(8,128)S(1)}, s32[32,128]{1,0:T(8,128)}, u32[]{:S(2)}) copy-start(s32[32,128]{1,0:T(8,128)} %lists_ref.3) | copy-start | bytes 49156
  38.9 10.1 %copy-start.2 = (f32[2,6]{1,0:T(2,128)S(1)}, f32[2,6]{1,0:T(2,128)}, u32[]{:S(2)}) copy-start(f32[2,6]{1,0:T(2,128)} %camera_ref.5) | copy-start | bytes 148
  38.9 10.1 %copy-start.3 = (s32[32]{0:T(128)S(1)}, s32[32]{0:T(128)}, u32[]{:S(2)}) copy-start(s32[32]{0:T(128)} %param.21) | copy-start | bytes 388

commit v5 on v4

--- a/solution.py
+++ b/solution.py
@@ -538,42 +538,44 @@
         for n, entry in enumerate(camera_frame(camera_ref, 0)):
             frame_ref[n] = entry
 
-    slot_grads = pick_eight(buffer_ref, inverse_ref[...])
-    rows = []
-    for g in range(8):
-        rows += turned([params_ref[8 * g : 8 * g + 8, LANES * c : LANES * (c + 1)] for c in range(8)])
-    frame = [frame_ref[n] for n in range(15)]
-    used = rows[:10] + [None] + rows[11:59]
-
-    def view_first(*leaves):
-        return footprint(list(leaves[:10]) + [None] + list(leaves[10:]), frame, *half)
-
-    made, pullback = jax.vjp(view_first, *(used[:10] + used[11:]))
-    ka, kb, kc = conic_of(*made[2:5])
-    ga, gb, gc = slot_grads[2], 0.5 * slot_grads[3], slot_grads[4]
-    left = [[ka * ga + kb * gb, ka * gb + kb * gc], [kb * ga + kc * gb, kb * gb + kc * gc]]
-    cover_grads = (
-        -(left[0][0] * ka + left[0][1] * kb),
-        -2.0 * (left[0][0] * kb + left[0][1] * kc),
-        -(left[1][0] * kb + left[1][1] * kc),
-    )
-    grads = list(pullback((slot_grads[0], slot_grads[1], *cover_grads, *slot_grads[6:])))
-    opacity_grad = slot_grads[5] * (1.0 - jax.nn.sigmoid(rows[10]))
-    grads = grads[:10] + [opacity_grad] + grads[10:] + [jnp.zeros((8, LANES), jnp.float32)] * 5
-    for g in range(8):
-        columns = turned(grads[8 * g : 8 * g + 8])
-        rate = rates_ref[8 * g : 8 * g + 8, :]
-        for c in range(8):
-            at = (slice(8 * g, 8 * g + 8), slice(LANES * c, LANES * (c + 1)))
-            gradient = columns[c]
-            first = 0.9 * first_ref[at] + 0.1 * gradient
-            second = 0.999 * second_ref[at] + 0.001 * gradient * gradient
-            value = params_ref[at] - rate * (first * (1.0 / bias_first)) / (
-                jnp.sqrt(second * (1.0 / bias_second)) + adam_epsilon
-            )
-            new_first_ref[at] = first
-            new_second_ref[at] = second
-            new_params_ref[at] = value
+    for h in range(params_ref.shape[1] // CHUNK):
+        left_edge = CHUNK * h
+        slot_grads = pick_eight(buffer_ref, inverse_ref[8 * h : 8 * h + 8, :])
+        rows = []
+        for g in range(8):
+            rows += turned([params_ref[8 * g : 8 * g + 8, left_edge + LANES * c : left_edge + LANES * (c + 1)] for c in range(8)])
+        frame = [frame_ref[n] for n in range(15)]
+        used = rows[:10] + [None] + rows[11:59]
+
+        def view_first(*leaves):
+            return footprint(list(leaves[:10]) + [None] + list(leaves[10:]), frame, *half)
+
+        made, pullback = jax.vjp(view_first, *(used[:10] + used[11:]))
+        ka, kb, kc = conic_of(*made[2:5])
+        ga, gb, gc = slot_grads[2], 0.5 * slot_grads[3], slot_grads[4]
+        left = [[ka * ga + kb * gb, ka * gb + kb * gc], [kb * ga + kc * gb, kb * gb + kc * gc]]
+        cover_grads = (
+            -(left[0][0] * ka + left[0][1] * kb),
+            -2.0 * (left[0][0] * kb + left[0][1] * kc),
+            -(left[1][0] * kb + left[1][1] * kc),
+        )
+        grads = list(pullback((slot_grads[0], slot_grads[1], *cover_grads, *slot_grads[6:])))
+        opacity_grad = slot_grads[5] * (1.0 - jax.nn.sigmoid(rows[10]))
+        grads = grads[:10] + [opacity_grad] + grads[10:] + [jnp.zeros((8, LANES), jnp.float32)] * 5
+        for g in range(8):
+            columns = turned(grads[8 * g : 8 * g + 8])
+            rate = rates_ref[8 * g : 8 * g + 8, :]
+            for c in range(8):
+                at = (slice(8 * g, 8 * g + 8), slice(left_edge + LANES * c, left_edge + LANES * (c + 1)))
+                gradient = columns[c]
+                first = 0.9 * first_ref[at] + 0.1 * gradient
+                second = 0.999 * second_ref[at] + 0.001 * gradient * gradient
+                value = params_ref[at] - rate * (first * (1.0 / bias_first)) / (
+                    jnp.sqrt(second * (1.0 / bias_second)) + adam_epsilon
+                )
+                new_first_ref[at] = first
+                new_second_ref[at] = second
+                new_params_ref[at] = value
 
 
 def render_kernel(
@@ -658,16 +660,17 @@
         compiler_params=linked(1),
         name="train",
     )(camera, gauss_params, slots_first, lists_first, tiles_first[None], jnp.transpose(targets, (1, 0, 2)))
-    block = pl.BlockSpec((64, CHUNK), lambda i: (0, i))
+    wide = 2
+    block = pl.BlockSpec((64, wide * CHUNK), lambda i: (0, i))
     new_params, new_first, new_second = pl.pallas_call(
         functools.partial(update_kernel, half=half),
-        grid=(steps,),
+        grid=(steps // wide,),
         out_shape=(f32(59, local), f32(59, local), f32(59, local)),
         in_specs=[
             scalars(),
             pl.BlockSpec((64, LANES), lambda i: (0, 0)),
             pl.BlockSpec(packet, lambda i: (0, 0, 0)),
-            pl.BlockSpec((8, LANES), lambda i: (i, 0)),
+            pl.BlockSpec((8 * wide, LANES), lambda i: (i, 0)),
             block, block, block,
         ],
         out_specs=(block, block, block),

time: 69.1 us -> 67.7 us (0.980)
  Pallas kernels: 67.4 us -> 66.1 us
    pallas_call x1, Pallas kernels: 10.1 us -> 8.76 us  [shards(): pl.pallas_call(functools.partial(update_kernel, half=half), grid=(steps /...]
where the time goes in v5:
time: 67.7 us; the launch traced here: 67.5 us
  Pallas kernels  66.1 us (98%)
  between operations  0.71 us (1%)
    pallas_call x1, Pallas kernels, shards(): pl.pallas_call(functools.partial(train_kernel, half=half), out_shape=(f32...  38.3 us
    pallas_call x1, Pallas kernels, shards(): pl.pallas_call(functools.partial(render_kernel, half=half), out_shape=f32...  19.1 us
    pallas_call x1, Pallas kernels, shards(): pl.pallas_call(functools.partial(update_kernel, half=half), grid=(steps /...  8.76 us

profile of v5, /device:TPU:1, one launch (start us, length us, event | category | flops | bytes accessed | tf_op | source)
XLA Modules:
  0.0 67.5 jit_solution(5013941960613048547)
XLA Ops:
  0.6 38.3 %train.1 = (f32[128,3,128]{2,1,0:T(4,128)}, s32[64,128]{1,0:T(8,128)}) custom-call(f32[2,6]{1,0:T(2,128)} %camera_ref.5, f32[59,8192]{1,0:T(8,128)} %params_ref.3, s32[32,128]{1,0:T(8,128)} %bitcast.10, s32[32,128]{1,0:T(8,128)} %lists_ref.2, s32[1,32]{1,0:T(1,128)} %bitcast.11, f32[3,32,256]{2,1,0:T(8,128)} %bitcast.9), custom_call_target="tpu_custom_call" | custom-call | tf_op jit(solution)/shard_map/train/pallas_call | solution.py:649
  38.9 0.0 copy-start
  38.9 0.0 copy-start.1
  38.9 0.0 copy-start.2
  38.9 0.0 copy-start.3
  39.0 8.8 %update.1 = (f32[59,8192]{1,0:T(8,128)}, f32[59,8192]{1,0:T(8,128)}, f32[59,8192]{1,0:T(8,128)}) custom-call(f32[2,6]{1,0:T(2,128)} %camera_ref.5, f32[64,128]{1,0:T(8,128)} %constant.2.clone.rates_ref, f32[128,3,128]{2,1,0:T(4,128)} %get-tuple-element.9.back_ref, s32[64,128]{1,0:T(8,128)} %get-tuple-element.10.inverse_ref, f32[59,8192]{1,0:T(8,128)} %params_ref.3, ...), custom_call_target="tpu_custom_call" | custom-call | tf_op jit(solution)/shard_map/update/pallas_call | solution.py:665
  47.7 0.0 copy-done
  47.7 0.0 copy-done.1
  47.7 0.0 copy-done.2
  47.7 0.0 copy-done.3
  47.7 19.1 %render.1 = f32[3,32,256]{2,1,0:T(8,128)S(1)} custom-call(f32[2,6]{1,0:T(2,128)S(1)} %copy-done.2, f32[59,8192]{1,0:T(8,128)} %get-tuple-element.18.params_ref, s32[32,128]{1,0:T(8,128)S(1)} %bitcast.7, s32[32,128]{1,0:T(8,128)S(1)} %copy-done.1, s32[1,32]{1,0:T(1,128)S(1)} %bitcast.8), custom_call_target="tpu_custom_call" | custom-call | tf_op jit(solution)/shard_map/render/pallas_call | solution.py:681
  66.8 0.6 copy.17
Async XLA Ops:
  38.9 8.8 %copy-start = (s32[1,4096]{1,0:T(1,128)S(1)}, s32[1,4096]{1,0:T(1,128)}, u32[]{:S(2)}) copy-start(s32[1,4096]{1,0:T(1,128)} %param.17) | copy-start | bytes 49156
  38.9 8.8 %copy-start.1 = (s32[32,128]{1,0:T(8,128)S(1)}, s32[32,128]{1,0:T(8,128)}, u32[]{:S(2)}) copy-start(s32[32,128]{1,0:T(8,128)} %lists_ref.3) | copy-start | bytes 49156
  38.9 8.8 %copy-start.2 = (f32[2,6]{1,0:T(2,128)S(1)}, f32[2,6]{1,0:T(2,128)}, u32[]{:S(2)}) copy-start(f32[2,6]{1,0:T(2,128)} %camera_ref.5) | copy-start | bytes 148
  38.9 8.8 %copy-start.3 = (s32[32]{0:T(128)S(1)}, s32[32]{0:T(128)}, u32[]{:S(2)}) copy-start(s32[32]{0:T(128)} %param.21) | copy-start | bytes 388

commit v6 on v5

--- a/solution.py
+++ b/solution.py
@@ -191,6 +191,51 @@
     return held
 
 
+def split_rows(source_ref, parts_ref):
+    half = source_ref.shape[1] // 2
+    for row in range(4):
+        rest = jnp.concatenate([source_ref[5 + row, :half], source_ref[5 + row, half:]], axis=1)
+        for part in range(3):
+            rounded = rest.astype(jnp.bfloat16)
+            start = (part * 4 + row) * half
+            parts_ref[start : start + half, :] = rounded
+            rest = rest - rounded.astype(jnp.float32)
+
+
+def pick_eight_split(source_ref, parts_ref, wanted):
+    blocks = source_ref.shape[1]
+    half = blocks // 2
+    high, low = wanted >> 7, wanted & 127
+    column = ((wanted >> (7 + half.bit_length() - 1)) << 7) | low
+    line = high & (half - 1)
+    line_id = lax.broadcasted_iota(jnp.int32, (half, 2 * LANES), 0)
+    column_id = lax.broadcasted_iota(jnp.int32, (2 * LANES, 2 * LANES), 0)
+    found = [[] for _ in range(4)]
+    for pair in range(4):
+
+        def joined(values):
+            return jnp.concatenate(
+                [values[2 * pair : 2 * pair + 1], values[2 * pair + 1 : 2 * pair + 2]], axis=1
+            )
+
+        choose = jnp.where(column_id == joined(column), 1.0, 0.0).astype(jnp.bfloat16)
+        hit = line_id == joined(line)
+        part = jnp.dot(parts_ref[...], choose, preferred_element_type=jnp.float32)
+        size = 4 * half
+        value = part[:size] + part[size : 2 * size] + part[2 * size :]
+        for row in range(4):
+            one = jnp.where(hit, value[row * half : (row + 1) * half], 0.0)
+            one = jnp.sum(one, axis=0, keepdims=True)
+            found[row] += [one[:, :LANES], one[:, LANES:]]
+    held = [jnp.zeros((8, LANES), jnp.float32)] * 5
+    for block in range(blocks):
+        here = high == block
+        for row in range(5):
+            source = jnp.broadcast_to(source_ref[row, block : block + 1, :], (8, LANES))
+            held[row] = jnp.where(here, lane_pick(source, low), held[row])
+    return held + [jnp.concatenate(rows, axis=0) for rows in found]
+
+
 def pick(source_ref, wanted_ref, picked_ref):
     def body(g, _):
         at = pl.ds(pl.multiple_of(g * 8, 8), 8)
@@ -257,7 +302,7 @@
 
 
 def deliver(
-    source_ref, wanted_ref, message_ref, landing_ref, sent, landed, ready, meanwhile
+    source_ref, parts_ref, wanted_ref, message_ref, landing_ref, sent, landed, ready, meanwhile
 ):
     me, devices = lax.axis_index("dev"), lax.axis_size("dev")
     share = devices // 4
@@ -273,10 +318,16 @@
             device_id_type=pl.DeviceIdType.MESH,
         )
 
+    if parts_ref is not None:
+        split_rows(source_ref, parts_ref)
     for ahead in (2, 1, 3, 0):
         g = lax.rem(home + ahead, 4)
         at = pl.ds(pl.multiple_of(g * 8, 8), 8)
-        pack_group(pick_eight(source_ref, wanted_ref[at, :]), message_ref, g)
+        if parts_ref is None:
+            values = pick_eight(source_ref, wanted_ref[at, :])
+        else:
+            values = pick_eight_split(source_ref, parts_ref, wanted_ref[at, :])
+        pack_group(values, message_ref, g)
         if ahead == 2 and ready is not None:
             ready()
 
@@ -429,7 +480,7 @@
 
 def train_kernel(
     camera_ref, params_ref, send_ref, lists_ref, tiles_ref, targets_ref, returned_ref, from_send_ref,
-    params_held, splats_ref, buffer_ref, picked_ref, rows_ref, alpha_ref, weight_ref, sums_ref,
+    params_held, splats_ref, parts_ref, buffer_ref, picked_ref, rows_ref, alpha_ref, weight_ref, sums_ref,
     miss_ref, message_ref, landing_ref, turn_ref, order_ref, from_list_ref, goals_ref,
     loaded, sent, landed, sent_back, landed_back, *, half,
 ):
@@ -440,7 +491,8 @@
         from_list_ref[...] = inverse_of(order_ref, 32)
 
     deliver(
-        splats_ref, send_ref, message_ref.at[0], landing_ref, sent, landed, greeted, before_landing
+        splats_ref, parts_ref, send_ref, message_ref.at[0], landing_ref, sent, landed,
+        greeted, before_landing,
     )
     unpack(landing_ref, buffer_ref)
     pick(buffer_ref, order_ref, picked_ref)
@@ -520,7 +572,7 @@
         from_send_ref[...] = inverse_of(send_ref, from_send_ref.shape[0])
 
     deliver(
-        buffer_ref, from_list_ref, message_ref.at[1], returned_ref, sent_back, landed_back,
+        buffer_ref, None, from_list_ref, message_ref.at[1], returned_ref, sent_back, landed_back,
         None, before_return,
     )
 
@@ -580,12 +632,12 @@
 
 def render_kernel(
     camera_ref, params_ref, send_ref, lists_ref, tiles_ref, image_ref,
-    params_held, splats_ref, buffer_ref, picked_ref, rows_ref, message_ref, landing_ref,
+    params_held, splats_ref, parts_ref, buffer_ref, picked_ref, rows_ref, message_ref, landing_ref,
     turn_ref, order_ref, loaded, sent, landed, *, half,
 ):
     project_all(1, camera_ref, params_ref, params_held, splats_ref, loaded, half)
     deliver(
-        splats_ref, send_ref, message_ref, landing_ref, sent, landed, greeted,
+        splats_ref, parts_ref, send_ref, message_ref, landing_ref, sent, landed, greeted,
         lambda: list_order(lists_ref, turn_ref, order_ref),
     )
     unpack(landing_ref, buffer_ref)
@@ -640,7 +692,10 @@
     packet = (devices, 3, LANES)
     links = [pltpu.SemaphoreType.DMA((2,)), pltpu.SemaphoreType.DMA((1,))]
     loading = pltpu.SemaphoreType.DMA((steps,))
-    held = [vmem((steps, 59, CHUNK)), vmem((9, blocks, LANES)), vmem((9, 32, LANES)), vmem((9, 32, LANES))]
+    held = [
+        vmem((steps, 59, CHUNK)), vmem((9, blocks, LANES)),
+        pltpu.VMEM((6 * blocks, 2 * LANES), jnp.bfloat16), vmem((9, 32, LANES)), vmem((9, 32, LANES)),
+    ]
     outside = pl.BlockSpec(memory_space=pltpu.HBM)
 
     def integers(*shape):

time: 67.7 us -> 66.8 us (0.987)
  Pallas kernels: 66.1 us -> 65.2 us
where the time goes in v6:
time: 66.8 us; the launch traced here: 66.6 us
  Pallas kernels  65.2 us (98%)
  between operations  0.71 us (1%)
  local copies, waits for them, and re-layouts  0.67 us (1%)
    pallas_call x1, Pallas kernels, shards(): pl.pallas_call(functools.partial(train_kernel, half=half), out_shape=(f32...  37.7 us
    pallas_call x1, Pallas kernels, shards(): pl.pallas_call(functools.partial(render_kernel, half=half), out_shape=f32...  18.7 us
    pallas_call x1, Pallas kernels, shards(): pl.pallas_call(functools.partial(update_kernel, half=half), grid=(steps /...  8.76 us

profile of v6, /device:TPU:1, one launch (start us, length us, event | category | flops | bytes accessed | tf_op | source)
XLA Modules:
  0.0 66.6 jit_solution(979779118596835214)
XLA Ops:
  0.6 37.7 %train.1 = (f32[128,3,128]{2,1,0:T(4,128)}, s32[64,128]{1,0:T(8,128)}) custom-call(f32[2,6]{1,0:T(2,128)} %camera_ref.5, f32[59,8192]{1,0:T(8,128)} %params_ref.3, s32[32,128]{1,0:T(8,128)} %bitcast.10, s32[32,128]{1,0:T(8,128)} %lists_ref.2, s32[1,32]{1,0:T(1,128)} %bitcast.11, f32[3,32,256]{2,1,0:T(8,128)} %bitcast.9), custom_call_target="tpu_custom_call" | custom-call | tf_op jit(solution)/shard_map/train/pallas_call | solution.py:704
  38.3 0.0 copy-start
  38.3 0.0 copy-start.1
  38.3 0.0 copy-start.2
  38.4 0.0 copy-start.3
  38.4 8.8 %update.1 = (f32[59,8192]{1,0:T(8,128)}, f32[59,8192]{1,0:T(8,128)}, f32[59,8192]{1,0:T(8,128)}) custom-call(f32[2,6]{1,0:T(2,128)} %camera_ref.5, f32[64,128]{1,0:T(8,128)} %constant.2.clone.rates_ref, f32[128,3,128]{2,1,0:T(4,128)} %get-tuple-element.9.back_ref, s32[64,128]{1,0:T(8,128)} %get-tuple-element.10.inverse_ref, f32[59,8192]{1,0:T(8,128)} %params_ref.3, ...), custom_call_target="tpu_custom_call" | custom-call | tf_op jit(solution)/shard_map/update/pallas_call | solution.py:720
  47.1 0.0 copy-done
  47.1 0.0 copy-done.1
  47.1 0.0 copy-done.2
  47.2 0.0 copy-done.3
  47.2 18.7 %render.1 = f32[3,32,256]{2,1,0:T(8,128)S(1)} custom-call(f32[2,6]{1,0:T(2,128)S(1)} %copy-done.2, f32[59,8192]{1,0:T(8,128)} %get-tuple-element.18.params_ref, s32[32,128]{1,0:T(8,128)S(1)} %bitcast.7, s32[32,128]{1,0:T(8,128)S(1)} %copy-done.1, s32[1,32]{1,0:T(1,128)S(1)} %bitcast.8), custom_call_target="tpu_custom_call" | custom-call | tf_op jit(solution)/shard_map/render/pallas_call | solution.py:736
  65.9 0.6 copy.17
Async XLA Ops:
  38.3 8.8 %copy-start = (s32[1,4096]{1,0:T(1,128)S(1)}, s32[1,4096]{1,0:T(1,128)}, u32[]{:S(2)}) copy-start(s32[1,4096]{1,0:T(1,128)} %param.17) | copy-start | bytes 49156
  38.3 8.8 %copy-start.1 = (s32[32,128]{1,0:T(8,128)S(1)}, s32[32,128]{1,0:T(8,128)}, u32[]{:S(2)}) copy-start(s32[32,128]{1,0:T(8,128)} %lists_ref.3) | copy-start | bytes 49156
  38.3 8.8 %copy-start.2 = (f32[2,6]{1,0:T(2,128)S(1)}, f32[2,6]{1,0:T(2,128)}, u32[]{:S(2)}) copy-start(f32[2,6]{1,0:T(2,128)} %camera_ref.5) | copy-start | bytes 148
  38.4 8.8 %copy-start.3 = (s32[32]{0:T(128)S(1)}, s32[32]{0:T(128)}, u32[]{:S(2)}) copy-start(s32[32]{0:T(128)} %param.21) | copy-start | bytes 388
